TPU v7x, 32 devices: a whole 2x2x4 slice. The times are simulated.
32 devices in a mesh: space: 8 (over z, y), shot: 4 (over x, core).
Axes of the slice: x: 2, y: 2, z: 4, core: 2. Of those that a mesh axis runs over, the one named last changes fastest.
Arguments:
- velocity: float32 [64, 192, 128], P('space'), may hold values from 1.5 to 4.5
- wave_now: float32 [4, 64, 192, 128], P('shot', 'space'), may hold values from -6 to 6
- wave_prev: float32 [4, 64, 192, 128], P('shot', 'space'), may hold values from -6 to 6
- adjoint_now: float32 [4, 64, 192, 128], P('shot', 'space'), may hold values from -6 to 6
- adjoint_prev: float32 [4, 64, 192, 128], P('shot', 'space'), may hold values from -6 to 6
- source_cells: int32 [4, 128], P('shot'), may hold values from 0 to 1572863, as said below
- wavelet: float32 [4, 10, 128], P('shot'), may hold values from -24 to 24
- receiver_cells: int32 [4096], P('space'), may hold values from 0 to 196607, as said below
- receiver_counts: int32 [8], P('space'), may hold values from 128 to 512, as said below
- observed: float32 [4, 10, 4096], P('shot', None, 'space'), may hold values from -24 to 24
Outputs:
- gradient: float32 [64, 192, 128], P('space', 'shot')
Inputs may be any that keep to these rules, and one draw needn't show every extreme that they name: `source_cells`: flat indices into the whole grid (first dimension slowest); the 128 cells of one shot group are distinct. `receiver_cells`: flat indices within one device's block of 8 x 192 x 128 cells (first dimension slowest); the 512 cells of one block are distinct. `receiver_counts`: the live slots of a block come first.
All inputs are finite; a program needn't handle non-finite values.
Results may differ from a plain program's by a relative error of at most 0.00002.
Values sent between devices are 32-bit elements; how exact they have to be, the bound alone decides.
A program may use at most 64 MiB of HBM per device.

v0:
```python
import jax
import jax.numpy as jnp
from jax import lax
from jax.sharding import PartitionSpec as P

TAPS = (-205.0 / 72.0, 8.0 / 5.0, -1.0 / 5.0, 8.0 / 315.0, -1.0 / 560.0)
COURANT = 0.09


def with_halo(block, sides, width):
    for axis, dim in sides:
        count = lax.axis_size(axis)
        forward = [(i, i + 1) for i in range(count - 1)]
        backward = [(target, source) for source, target in forward]
        low = lax.ppermute(
            lax.slice_in_dim(block, block.shape[dim] - width, None, axis=dim), axis, forward
        )
        high = lax.ppermute(lax.slice_in_dim(block, 0, width, axis=dim), axis, backward)
        block = jnp.concatenate([low, block, high], axis=dim)
    return block


def laplace(widened):
    length_x = widened.shape[0] - 8
    extent_y = widened.shape[1]
    extent_z = widened.shape[2]
    padded = jnp.pad(widened, ((0, 0), (4, 4), (4, 4)))
    centre = widened[4 : 4 + length_x]
    result = 3.0 * TAPS[0] * centre
    for distance in range(1, 5):
        beside_all = (
            padded[4 + distance : 4 + distance + length_x, 4 : 4 + extent_y, 4 : 4 + extent_z]
            + padded[4 - distance : 4 - distance + length_x, 4 : 4 + extent_y, 4 : 4 + extent_z]
        )
        beside_all = (
            beside_all
            + padded[4 : 4 + length_x, 4 + distance : 4 + distance + extent_y, 4 : 4 + extent_z]
            + padded[4 : 4 + length_x, 4 - distance : 4 - distance + extent_y, 4 : 4 + extent_z]
        )
        beside_all = (
            beside_all
            + padded[4 : 4 + length_x, 4 : 4 + extent_y, 4 + distance : 4 + distance + extent_z]
            + padded[4 : 4 + length_x, 4 : 4 + extent_y, 4 - distance : 4 - distance + extent_z]
        )
        result = result + TAPS[distance] * beside_all
    return result


def edge_layers(field):
    return with_halo(field, (("space", 0),), 4)


def add_at(field, target, amounts):
    size_all = field.size
    inside = (target >= 0) & (target < size_all)
    flat_field = (
        field.reshape(-1).at[jnp.where(inside, target, 0)].add(jnp.where(inside, amounts, 0.0))
    )
    return flat_field.reshape(field.shape)


def per_device(
    velocity,
    wave_now,
    wave_prev,
    adjoint_now,
    adjoint_prev,
    source_cells,
    wavelet,
    receiver_cells,
    receiver_counts,
    observed,
):
    extent_x, extent_y, extent_z = velocity.shape
    plane_cells = extent_y * extent_z
    courant_sq = (COURANT * velocity) ** 2
    position = lax.axis_index("space")
    local_sources = source_cells[0] - position * (extent_x * plane_cells)
    pulses = wavelet[0]

    def forward(carried, source_pulse):
        current, former = carried
        latest = 2.0 * current - former + courant_sq * laplace(edge_layers(current))
        latest = add_at(latest, local_sources, source_pulse)
        acceleration = latest - 2.0 * current + former
        return ((latest, current), (acceleration, latest.reshape(-1)[receiver_cells]))

    _, (accelerations, traces) = lax.scan(forward, (wave_now[0], wave_prev[0]), pulses)
    live_slots = (jnp.arange(receiver_cells.shape[0], dtype=jnp.int32) < receiver_counts[0]).astype(
        jnp.float32
    )
    misfit = (traces - observed[0]) * live_slots

    def backward(carried, inputs):
        following, furthest, imaging = carried
        acceleration, residual = inputs
        earlier = 2.0 * following - furthest + courant_sq * laplace(edge_layers(following))
        earlier = earlier.reshape(-1).at[receiver_cells].add(residual).reshape(velocity.shape)
        return ((earlier, following, imaging + earlier * acceleration), None)

    empty_field = jnp.zeros_like(velocity)
    (_, _, imaging), _ = lax.scan(
        backward,
        (adjoint_now[0], adjoint_prev[0], empty_field),
        (accelerations, misfit),
        reverse=True,
    )
    band_rows = extent_y // lax.axis_size("shot")
    offset = lax.axis_index("shot") * band_rows
    factor = lax.dynamic_slice_in_dim(-2.0 / velocity**3, offset, band_rows, 1)
    own_band = lax.psum_scatter(imaging, "shot", scatter_dimension=1, tiled=True)
    return factor * own_band


def solution(mesh):
    in_specs = (
        P("space", None, None),
        P("shot", "space", None, None),
        P("shot", "space", None, None),
        P("shot", "space", None, None),
        P("shot", "space", None, None),
        P("shot", None),
        P("shot", None, None),
        P("space"),
        P("space"),
        P("shot", None, "space"),
    )
    out_specs = P("space", "shot", None)
    return jax.shard_map(
        per_device, mesh=mesh, in_specs=in_specs, out_specs=out_specs, check_vma=False
    )
```

profile of v0, /device:TPU:4, one launch (start us, length us, event | category | flops | bytes accessed | tf_op | source)
XLA Modules:
  0.0 753.9 jit_solution(10697863546223866510)
XLA Ops:
  12.2 363.2 %while.37 = (s32[]{:T(128)}, f32[8,192,128]{2,1,0:T(8,128)S(1)}, f32[8,192,128]{2,1,0:T(8,128)}, f32[10,8,192,128]{3,2,1,0:T(8,128)}, f32[10,512]{1,0:T(8,128)},...) while((s32[]{:T(128)}, f32[8,192,128]{2,1,0:T(8,128)S(1)}, ...), condition=%wide.region_2.3_spmd, body=%wide.region_0.2_spmd.sunk | while | flops 13609986 | bytes 43449096 | solution.py:88
  20.8 13.7 %collective-permute-done.1 = f32[4,192,128]{2,1,0:T(8,128)S(1)} collective-permute-done((f32[4,192,128]{2,1,0:T(8,128)}, f32[4,192,128]{2,1,0:T(8,128)S(1)}, u32[]{:S(2)}, u32[]{:S(2)}) %collective-permute-start.1) | collective-permute-done | bytes 393248 | tf_op jit(solution)/shard_map/while/body/eval_jaxpr/ppermute | solution.py:15
  49.2 4.0 collective-permute-start.1
  56.9 12.7 %collective-permute-done.1 = f32[4,192,128]{2,1,0:T(8,128)S(1)} collective-permute-done((f32[4,192,128]{2,1,0:T(8,128)}, f32[4,192,128]{2,1,0:T(8,128)S(1)}, u32[]{:S(2)}, u32[]{:S(2)}) %collective-permute-start.1) | collective-permute-done | bytes 393248 | tf_op jit(solution)/shard_map/while/body/eval_jaxpr/ppermute | solution.py:15
  84.4 5.6 collective-permute-start.1
  93.9 10.2 %collective-permute-done.1 = f32[4,192,128]{2,1,0:T(8,128)S(1)} collective-permute-done((f32[4,192,128]{2,1,0:T(8,128)}, f32[4,192,128]{2,1,0:T(8,128)S(1)}, u32[]{:S(2)}, u32[]{:S(2)}) %collective-permute-start.1) | collective-permute-done | bytes 393248 | tf_op jit(solution)/shard_map/while/body/eval_jaxpr/ppermute | solution.py:15
  118.8 8.2 %collective-permute-start.1 = (f32[4,192,128]{2,1,0:T(8,128)}, f32[4,192,128]{2,1,0:T(8,128)S(1)}, u32[]{:S(2)}, u32[]{:S(2)}) collective-permute-start(f32[4,192,128]{2,1,0:T(8,128)} %get-tuple-element.457), channel_id=1, source_target_pairs={{0,4},{4,8},{8,12},{12,16},{16,20},{20,24},{24,28},{1,5},{5,9},{9,... | collective-permute-start | bytes 1179656 | tf_op jit(solution)/shard_map/while/body/eval_jaxpr/ppermute | solution.py:15
  130.7 5.1 collective-permute-done.1
  136.0 4.5 collective-permute-done
  154.9 8.9 %collective-permute-start.1 = (f32[4,192,128]{2,1,0:T(8,128)}, f32[4,192,128]{2,1,0:T(8,128)S(1)}, u32[]{:S(2)}, u32[]{:S(2)}) collective-permute-start(f32[4,192,128]{2,1,0:T(8,128)} %get-tuple-element.457), channel_id=1, source_target_pairs={{0,4},{4,8},{8,12},{12,16},{16,20},{20,24},{24,28},{1,5},{5,9},{9,... | collective-permute-start | bytes 1179656 | tf_op jit(solution)/shard_map/while/body/eval_jaxpr/ppermute | solution.py:15
  167.6 5.1 collective-permute-done.1
  172.9 4.5 collective-permute-done
  191.8 8.9 %collective-permute-start.1 = (f32[4,192,128]{2,1,0:T(8,128)}, f32[4,192,128]{2,1,0:T(8,128)S(1)}, u32[]{:S(2)}, u32[]{:S(2)}) collective-permute-start(f32[4,192,128]{2,1,0:T(8,128)} %get-tuple-element.457), channel_id=1, source_target_pairs={{0,4},{4,8},{8,12},{12,16},{16,20},{20,24},{24,28},{1,5},{5,9},{9,... | collective-permute-start | bytes 1179656 | tf_op jit(solution)/shard_map/while/body/eval_jaxpr/ppermute | solution.py:15
  204.5 5.1 collective-permute-done.1
  209.8 4.5 collective-permute-done
  228.7 8.9 %collective-permute-start.1 = (f32[4,192,128]{2,1,0:T(8,128)}, f32[4,192,128]{2,1,0:T(8,128)S(1)}, u32[]{:S(2)}, u32[]{:S(2)}) collective-permute-start(f32[4,192,128]{2,1,0:T(8,128)} %get-tuple-element.457), channel_id=1, source_target_pairs={{0,4},{4,8},{8,12},{12,16},{16,20},{20,24},{24,28},{1,5},{5,9},{9,... | collective-permute-start | bytes 1179656 | tf_op jit(solution)/shard_map/while/body/eval_jaxpr/ppermute | solution.py:15
  241.4 5.1 collective-permute-done.1
  246.7 4.5 collective-permute-done
  265.6 8.9 %collective-permute-start.1 = (f32[4,192,128]{2,1,0:T(8,128)}, f32[4,192,128]{2,1,0:T(8,128)S(1)}, u32[]{:S(2)}, u32[]{:S(2)}) collective-permute-start(f32[4,192,128]{2,1,0:T(8,128)} %get-tuple-element.457), channel_id=1, source_target_pairs={{0,4},{4,8},{8,12},{12,16},{16,20},{20,24},{24,28},{1,5},{5,9},{9,... | collective-permute-start | bytes 1179656 | tf_op jit(solution)/shard_map/while/body/eval_jaxpr/ppermute | solution.py:15
  278.3 5.1 collective-permute-done.1
  283.6 4.5 collective-permute-done
  302.5 8.9 %collective-permute-start.1 = (f32[4,192,128]{2,1,0:T(8,128)}, f32[4,192,128]{2,1,0:T(8,128)S(1)}, u32[]{:S(2)}, u32[]{:S(2)}) collective-permute-start(f32[4,192,128]{2,1,0:T(8,128)} %get-tuple-element.457), channel_id=1, source_target_pairs={{0,4},{4,8},{8,12},{12,16},{16,20},{20,24},{24,28},{1,5},{5,9},{9,... | collective-permute-start | bytes 1179656 | tf_op jit(solution)/shard_map/while/body/eval_jaxpr/ppermute | solution.py:15
  315.2 5.1 collective-permute-done.1
  320.5 4.5 collective-permute-done
  339.4 8.9 %collective-permute-start.1 = (f32[4,192,128]{2,1,0:T(8,128)}, f32[4,192,128]{2,1,0:T(8,128)S(1)}, u32[]{:S(2)}, u32[]{:S(2)}) collective-permute-start(f32[4,192,128]{2,1,0:T(8,128)} %get-tuple-element.457), channel_id=1, source_target_pairs={{0,4},{4,8},{8,12},{12,16},{16,20},{20,24},{24,28},{1,5},{5,9},{9,... | collective-permute-start | bytes 1179656 | tf_op jit(solution)/shard_map/while/body/eval_jaxpr/ppermute | solution.py:15
  352.1 5.1 collective-permute-done.1
  357.4 4.5 collective-permute-done
  376.8 339.6 %while.38 = (s32[]{:T(128)}, f32[8,192,128]{2,1,0:T(8,128)S(1)}, f32[8,192,128]{2,1,0:T(8,128)}, f32[8,192,128]{2,1,0:T(8,128)}, f32[8,192,128]{2,1,0:T(8,128)S(...) while((s32[]{:T(128)}, f32[8,192,128]{2,1,0:T(8,128)S(1)}, ...), condition=%wide.region_5.6_spmd.clone, body=%wide.region_3.5_spmd.clone.sunk | while | flops 13607940 | bytes 49729836 | solution.py:102
  376.9 8.9 %collective-permute-start.3 = (f32[4,192,128]{2,1,0:T(8,128)S(1)}, f32[4,192,128]{2,1,0:T(8,128)S(1)}, u32[]{:S(2)}, u32[]{:S(2)}) collective-permute-start(f32[4,192,128]{2,1,0:T(8,128)S(1)} %get-tuple-element.469), channel_id=1, source_target_pairs={{0,4},{4,8},{8,12},{12,16},{16,20},{20,24},{24,28},{1,5},{5,9},{9,... | collective-permute-start | bytes 1179656 | tf_op jit(solution)/shard_map/while/body/eval_jaxpr/ppermute | solution.py:15
  388.5 5.9 collective-permute-done.3
  394.6 4.8 collective-permute-done.2
  411.0 8.7 %collective-permute-start.3 = (f32[4,192,128]{2,1,0:T(8,128)S(1)}, f32[4,192,128]{2,1,0:T(8,128)S(1)}, u32[]{:S(2)}, u32[]{:S(2)}) collective-permute-start(f32[4,192,128]{2,1,0:T(8,128)S(1)} %get-tuple-element.469), channel_id=1, source_target_pairs={{0,4},{4,8},{8,12},{12,16},{16,20},{20,24},{24,28},{1,5},{5,9},{9,... | collective-permute-start | bytes 1179656 | tf_op jit(solution)/shard_map/while/body/eval_jaxpr/ppermute | solution.py:15
  422.4 5.9 collective-permute-done.3
  428.5 4.8 collective-permute-done.2
  438.5 3.7 scatter_fusion.1
  445.0 8.7 %collective-permute-start.3 = (f32[4,192,128]{2,1,0:T(8,128)S(1)}, f32[4,192,128]{2,1,0:T(8,128)S(1)}, u32[]{:S(2)}, u32[]{:S(2)}) collective-permute-start(f32[4,192,128]{2,1,0:T(8,128)S(1)} %get-tuple-element.469), channel_id=1, source_target_pairs={{0,4},{4,8},{8,12},{12,16},{16,20},{20,24},{24,28},{1,5},{5,9},{9,... | collective-permute-start | bytes 1179656 | tf_op jit(solution)/shard_map/while/body/eval_jaxpr/ppermute | solution.py:15
  456.4 5.9 collective-permute-done.3
  462.5 4.8 collective-permute-done.2
  472.4 3.7 scatter_fusion.1
  478.9 8.7 %collective-permute-start.3 = (f32[4,192,128]{2,1,0:T(8,128)S(1)}, f32[4,192,128]{2,1,0:T(8,128)S(1)}, u32[]{:S(2)}, u32[]{:S(2)}) collective-permute-start(f32[4,192,128]{2,1,0:T(8,128)S(1)} %get-tuple-element.469), channel_id=1, source_target_pairs={{0,4},{4,8},{8,12},{12,16},{16,20},{20,24},{24,28},{1,5},{5,9},{9,... | collective-permute-start | bytes 1179656 | tf_op jit(solution)/shard_map/while/body/eval_jaxpr/ppermute | solution.py:15
  490.3 5.9 collective-permute-done.3
  496.4 4.8 collective-permute-done.2
  506.4 3.7 scatter_fusion.1
  512.8 8.7 %collective-permute-start.3 = (f32[4,192,128]{2,1,0:T(8,128)S(1)}, f32[4,192,128]{2,1,0:T(8,128)S(1)}, u32[]{:S(2)}, u32[]{:S(2)}) collective-permute-start(f32[4,192,128]{2,1,0:T(8,128)S(1)} %get-tuple-element.469), channel_id=1, source_target_pairs={{0,4},{4,8},{8,12},{12,16},{16,20},{20,24},{24,28},{1,5},{5,9},{9,... | collective-permute-start | bytes 1179656 | tf_op jit(solution)/shard_map/while/body/eval_jaxpr/ppermute | solution.py:15
  524.2 5.9 collective-permute-done.3
  530.3 4.8 collective-permute-done.2
  540.3 3.7 scatter_fusion.1
  546.8 8.7 %collective-permute-start.3 = (f32[4,192,128]{2,1,0:T(8,128)S(1)}, f32[4,192,128]{2,1,0:T(8,128)S(1)}, u32[]{:S(2)}, u32[]{:S(2)}) collective-permute-start(f32[4,192,128]{2,1,0:T(8,128)S(1)} %get-tuple-element.469), channel_id=1, source_target_pairs={{0,4},{4,8},{8,12},{12,16},{16,20},{20,24},{24,28},{1,5},{5,9},{9,... | collective-permute-start | bytes 1179656 | tf_op jit(solution)/shard_map/while/body/eval_jaxpr/ppermute | solution.py:15
  558.2 5.9 collective-permute-done.3
  564.3 4.8 collective-permute-done.2
  580.7 8.7 %collective-permute-start.3 = (f32[4,192,128]{2,1,0:T(8,128)S(1)}, f32[4,192,128]{2,1,0:T(8,128)S(1)}, u32[]{:S(2)}, u32[]{:S(2)}) collective-permute-start(f32[4,192,128]{2,1,0:T(8,128)S(1)} %get-tuple-element.469), channel_id=1, source_target_pairs={{0,4},{4,8},{8,12},{12,16},{16,20},{20,24},{24,28},{1,5},{5,9},{9,... | collective-permute-start | bytes 1179656 | tf_op jit(solution)/shard_map/while/body/eval_jaxpr/ppermute | solution.py:15
  592.1 5.9 collective-permute-done.3
  598.2 4.8 collective-permute-done.2
  608.2 3.7 scatter_fusion.1
  614.7 8.7 %collective-permute-start.3 = (f32[4,192,128]{2,1,0:T(8,128)S(1)}, f32[4,192,128]{2,1,0:T(8,128)S(1)}, u32[]{:S(2)}, u32[]{:S(2)}) collective-permute-start(f32[4,192,128]{2,1,0:T(8,128)S(1)} %get-tuple-element.469), channel_id=1, source_target_pairs={{0,4},{4,8},{8,12},{12,16},{16,20},{20,24},{24,28},{1,5},{5,9},{9,... | collective-permute-start | bytes 1179656 | tf_op jit(solution)/shard_map/while/body/eval_jaxpr/ppermute | solution.py:15
  626.0 5.9 collective-permute-done.3
  632.1 4.8 collective-permute-done.2
  648.6 8.7 %collective-permute-start.3 = (f32[4,192,128]{2,1,0:T(8,128)S(1)}, f32[4,192,128]{2,1,0:T(8,128)S(1)}, u32[]{:S(2)}, u32[]{:S(2)}) collective-permute-start(f32[4,192,128]{2,1,0:T(8,128)S(1)} %get-tuple-element.469), channel_id=1, source_target_pairs={{0,4},{4,8},{8,12},{12,16},{16,20},{20,24},{24,28},{1,5},{5,9},{9,... | collective-permute-start | bytes 1179656 | tf_op jit(solution)/shard_map/while/body/eval_jaxpr/ppermute | solution.py:15
  660.0 5.9 collective-permute-done.3
  666.1 4.8 collective-permute-done.2
  682.5 8.7 %collective-permute-start.3 = (f32[4,192,128]{2,1,0:T(8,128)S(1)}, f32[4,192,128]{2,1,0:T(8,128)S(1)}, u32[]{:S(2)}, u32[]{:S(2)}) collective-permute-start(f32[4,192,128]{2,1,0:T(8,128)S(1)} %get-tuple-element.469), channel_id=1, source_target_pairs={{0,4},{4,8},{8,12},{12,16},{16,20},{20,24},{24,28},{1,5},{5,9},{9,... | collective-permute-start | bytes 1179656 | tf_op jit(solution)/shard_map/while/body/eval_jaxpr/ppermute | solution.py:15
  693.9 5.9 collective-permute-done.3
  700.0 4.8 collective-permute-done.2
  716.4 28.8 %reduce-scatter.2.cloned.1.call-done = f32[8,48,128]{2,1,0:T(8,128)} async-done(((f32[8,192,128]{2,1,0:T(8,128)}), f32[8,48,128]{2,1,0:T(8,128)}) %reduce-scatter.2.cloned.1.call-update) | async-done | bytes 196624 | tf_op jit(solution)/shard_map/reduce_scatter | solution.py:111
  (426 shorter events, 321.0 us)
Async XLA Ops:
  6.5 738.7 %reduce-scatter.2.cloned.1.call-start = ((), (), s32[]{:S(2)}) async-start(), calls=%async_computation.1 | async-start | bytes 983040 | tf_op jit(solution)/shard_map/reduce_scatter | solution.py:111
  6.5 5.1 copy-start.11
  6.5 5.7 copy-start
  6.6 5.7 copy-start.8
  12.2 364.6 %copy-start.1 = (f32[1,8,192,128]{3,2,1,0:T(8,128)S(1)}, f32[1,8,192,128]{3,2,1,0:T(8,128)}, u32[]{:S(2)}) copy-start(f32[1,8,192,128]{3,2,1,0:T(8,128)} %param.17) | copy-start | bytes 2359300
  13.0 21.4 %collective-permute-start.1 = (f32[4,192,128]{2,1,0:T(8,128)}, f32[4,192,128]{2,1,0:T(8,128)S(1)}, u32[]{:S(2)}, u32[]{:S(2)}) collective-permute-start(f32[4,192,128]{2,1,0:T(8,128)} %get-tuple-element.457), channel_id=1, source_target_pairs={{0,4},{4,8},{8,12},{12,16},{16,20},{20,24},{24,28},{1,5},{5,9},{9,... | collective-permute-start | bytes 1179656 | tf_op jit(solution)/shard_map/while/body/eval_jaxpr/ppermute | solution.py:15
  16.5 18.1 %collective-permute-start = (f32[4,192,128]{2,1,0:T(8,128)S(1)}, f32[4,192,128]{2,1,0:T(8,128)S(1)}, u32[]{:S(2)}, u32[]{:S(2)}) collective-permute-start(f32[4,192,128]{2,1,0:T(8,128)S(1)} %get-tuple-element.456), channel_id=1, source_target_pairs={{4,0},{8,4},{12,8},{16,12},{20,16},{24,20},{28,24},{5,1},{9,5},{13... | collective-permute-start | bytes 1179656 | tf_op jit(solution)/shard_map/while/body/eval_jaxpr/ppermute | solution.py:18
  49.2 20.5 %collective-permute-start.1 = (f32[4,192,128]{2,1,0:T(8,128)}, f32[4,192,128]{2,1,0:T(8,128)S(1)}, u32[]{:S(2)}, u32[]{:S(2)}) collective-permute-start(f32[4,192,128]{2,1,0:T(8,128)} %get-tuple-element.457), channel_id=1, source_target_pairs={{0,4},{4,8},{8,12},{12,16},{16,20},{20,24},{24,28},{1,5},{5,9},{9,... | collective-permute-start | bytes 1179656 | tf_op jit(solution)/shard_map/while/body/eval_jaxpr/ppermute | solution.py:15
  53.2 16.7 %collective-permute-start = (f32[4,192,128]{2,1,0:T(8,128)S(1)}, f32[4,192,128]{2,1,0:T(8,128)S(1)}, u32[]{:S(2)}, u32[]{:S(2)}) collective-permute-start(f32[4,192,128]{2,1,0:T(8,128)S(1)} %get-tuple-element.456), channel_id=1, source_target_pairs={{4,0},{8,4},{12,8},{16,12},{20,16},{24,20},{28,24},{5,1},{9,5},{13... | collective-permute-start | bytes 1179656 | tf_op jit(solution)/shard_map/while/body/eval_jaxpr/ppermute | solution.py:18
  84.4 19.6 %collective-permute-start.1 = (f32[4,192,128]{2,1,0:T(8,128)}, f32[4,192,128]{2,1,0:T(8,128)S(1)}, u32[]{:S(2)}, u32[]{:S(2)}) collective-permute-start(f32[4,192,128]{2,1,0:T(8,128)} %get-tuple-element.457), channel_id=1, source_target_pairs={{0,4},{4,8},{8,12},{12,16},{16,20},{20,24},{24,28},{1,5},{5,9},{9,... | collective-permute-start | bytes 1179656 | tf_op jit(solution)/shard_map/while/body/eval_jaxpr/ppermute | solution.py:15
  90.1 14.2 %collective-permute-start = (f32[4,192,128]{2,1,0:T(8,128)S(1)}, f32[4,192,128]{2,1,0:T(8,128)S(1)}, u32[]{:S(2)}, u32[]{:S(2)}) collective-permute-start(f32[4,192,128]{2,1,0:T(8,128)S(1)} %get-tuple-element.456), channel_id=1, source_target_pairs={{4,0},{8,4},{12,8},{16,12},{20,16},{24,20},{28,24},{5,1},{9,5},{13... | collective-permute-start | bytes 1179656 | tf_op jit(solution)/shard_map/while/body/eval_jaxpr/ppermute | solution.py:18
  118.8 17.1 %collective-permute-start.1 = (f32[4,192,128]{2,1,0:T(8,128)}, f32[4,192,128]{2,1,0:T(8,128)S(1)}, u32[]{:S(2)}, u32[]{:S(2)}) collective-permute-start(f32[4,192,128]{2,1,0:T(8,128)} %get-tuple-element.457), channel_id=1, source_target_pairs={{0,4},{4,8},{8,12},{12,16},{16,20},{20,24},{24,28},{1,5},{5,9},{9,... | collective-permute-start | bytes 1179656 | tf_op jit(solution)/shard_map/while/body/eval_jaxpr/ppermute | solution.py:15
  127.0 13.6 %collective-permute-start = (f32[4,192,128]{2,1,0:T(8,128)S(1)}, f32[4,192,128]{2,1,0:T(8,128)S(1)}, u32[]{:S(2)}, u32[]{:S(2)}) collective-permute-start(f32[4,192,128]{2,1,0:T(8,128)S(1)} %get-tuple-element.456), channel_id=1, source_target_pairs={{4,0},{8,4},{12,8},{16,12},{20,16},{24,20},{28,24},{5,1},{9,5},{13... | collective-permute-start | bytes 1179656 | tf_op jit(solution)/shard_map/while/body/eval_jaxpr/ppermute | solution.py:18
  136.0 5.4 copy-start.2
  154.9 17.8 %collective-permute-start.1 = (f32[4,192,128]{2,1,0:T(8,128)}, f32[4,192,128]{2,1,0:T(8,128)S(1)}, u32[]{:S(2)}, u32[]{:S(2)}) collective-permute-start(f32[4,192,128]{2,1,0:T(8,128)} %get-tuple-element.457), channel_id=1, source_target_pairs={{0,4},{4,8},{8,12},{12,16},{16,20},{20,24},{24,28},{1,5},{5,9},{9,... | collective-permute-start | bytes 1179656 | tf_op jit(solution)/shard_map/while/body/eval_jaxpr/ppermute | solution.py:15
  163.8 13.6 %collective-permute-start = (f32[4,192,128]{2,1,0:T(8,128)S(1)}, f32[4,192,128]{2,1,0:T(8,128)S(1)}, u32[]{:S(2)}, u32[]{:S(2)}) collective-permute-start(f32[4,192,128]{2,1,0:T(8,128)S(1)} %get-tuple-element.456), channel_id=1, source_target_pairs={{4,0},{8,4},{12,8},{16,12},{20,16},{24,20},{28,24},{5,1},{9,5},{13... | collective-permute-start | bytes 1179656 | tf_op jit(solution)/shard_map/while/body/eval_jaxpr/ppermute | solution.py:18
  172.9 5.4 copy-start.2
  191.8 17.8 %collective-permute-start.1 = (f32[4,192,128]{2,1,0:T(8,128)}, f32[4,192,128]{2,1,0:T(8,128)S(1)}, u32[]{:S(2)}, u32[]{:S(2)}) collective-permute-start(f32[4,192,128]{2,1,0:T(8,128)} %get-tuple-element.457), channel_id=1, source_target_pairs={{0,4},{4,8},{8,12},{12,16},{16,20},{20,24},{24,28},{1,5},{5,9},{9,... | collective-permute-start | bytes 1179656 | tf_op jit(solution)/shard_map/while/body/eval_jaxpr/ppermute | solution.py:15
  200.7 13.6 %collective-permute-start = (f32[4,192,128]{2,1,0:T(8,128)S(1)}, f32[4,192,128]{2,1,0:T(8,128)S(1)}, u32[]{:S(2)}, u32[]{:S(2)}) collective-permute-start(f32[4,192,128]{2,1,0:T(8,128)S(1)} %get-tuple-element.456), channel_id=1, source_target_pairs={{4,0},{8,4},{12,8},{16,12},{20,16},{24,20},{28,24},{5,1},{9,5},{13... | collective-permute-start | bytes 1179656 | tf_op jit(solution)/shard_map/while/body/eval_jaxpr/ppermute | solution.py:18
  209.8 5.4 copy-start.2
  228.7 17.8 %collective-permute-start.1 = (f32[4,192,128]{2,1,0:T(8,128)}, f32[4,192,128]{2,1,0:T(8,128)S(1)}, u32[]{:S(2)}, u32[]{:S(2)}) collective-permute-start(f32[4,192,128]{2,1,0:T(8,128)} %get-tuple-element.457), channel_id=1, source_target_pairs={{0,4},{4,8},{8,12},{12,16},{16,20},{20,24},{24,28},{1,5},{5,9},{9,... | collective-permute-start | bytes 1179656 | tf_op jit(solution)/shard_map/while/body/eval_jaxpr/ppermute | solution.py:15
  237.6 13.6 %collective-permute-start = (f32[4,192,128]{2,1,0:T(8,128)S(1)}, f32[4,192,128]{2,1,0:T(8,128)S(1)}, u32[]{:S(2)}, u32[]{:S(2)}) collective-permute-start(f32[4,192,128]{2,1,0:T(8,128)S(1)} %get-tuple-element.456), channel_id=1, source_target_pairs={{4,0},{8,4},{12,8},{16,12},{20,16},{24,20},{28,24},{5,1},{9,5},{13... | collective-permute-start | bytes 1179656 | tf_op jit(solution)/shard_map/while/body/eval_jaxpr/ppermute | solution.py:18
  246.7 5.4 copy-start.2
  265.6 17.8 %collective-permute-start.1 = (f32[4,192,128]{2,1,0:T(8,128)}, f32[4,192,128]{2,1,0:T(8,128)S(1)}, u32[]{:S(2)}, u32[]{:S(2)}) collective-permute-start(f32[4,192,128]{2,1,0:T(8,128)} %get-tuple-element.457), channel_id=1, source_target_pairs={{0,4},{4,8},{8,12},{12,16},{16,20},{20,24},{24,28},{1,5},{5,9},{9,... | collective-permute-start | bytes 1179656 | tf_op jit(solution)/shard_map/while/body/eval_jaxpr/ppermute | solution.py:15
  274.5 13.6 %collective-permute-start = (f32[4,192,128]{2,1,0:T(8,128)S(1)}, f32[4,192,128]{2,1,0:T(8,128)S(1)}, u32[]{:S(2)}, u32[]{:S(2)}) collective-permute-start(f32[4,192,128]{2,1,0:T(8,128)S(1)} %get-tuple-element.456), channel_id=1, source_target_pairs={{4,0},{8,4},{12,8},{16,12},{20,16},{24,20},{28,24},{5,1},{9,5},{13... | collective-permute-start | bytes 1179656 | tf_op jit(solution)/shard_map/while/body/eval_jaxpr/ppermute | solution.py:18
  283.6 5.4 copy-start.2
  302.5 17.8 %collective-permute-start.1 = (f32[4,192,128]{2,1,0:T(8,128)}, f32[4,192,128]{2,1,0:T(8,128)S(1)}, u32[]{:S(2)}, u32[]{:S(2)}) collective-permute-start(f32[4,192,128]{2,1,0:T(8,128)} %get-tuple-element.457), channel_id=1, source_target_pairs={{0,4},{4,8},{8,12},{12,16},{16,20},{20,24},{24,28},{1,5},{5,9},{9,... | collective-permute-start | bytes 1179656 | tf_op jit(solution)/shard_map/while/body/eval_jaxpr/ppermute | solution.py:15
  311.4 13.6 %collective-permute-start = (f32[4,192,128]{2,1,0:T(8,128)S(1)}, f32[4,192,128]{2,1,0:T(8,128)S(1)}, u32[]{:S(2)}, u32[]{:S(2)}) collective-permute-start(f32[4,192,128]{2,1,0:T(8,128)S(1)} %get-tuple-element.456), channel_id=1, source_target_pairs={{4,0},{8,4},{12,8},{16,12},{20,16},{24,20},{28,24},{5,1},{9,5},{13... | collective-permute-start | bytes 1179656 | tf_op jit(solution)/shard_map/while/body/eval_jaxpr/ppermute | solution.py:18
  320.5 5.4 copy-start.2
  339.4 17.8 %collective-permute-start.1 = (f32[4,192,128]{2,1,0:T(8,128)}, f32[4,192,128]{2,1,0:T(8,128)S(1)}, u32[]{:S(2)}, u32[]{:S(2)}) collective-permute-start(f32[4,192,128]{2,1,0:T(8,128)} %get-tuple-element.457), channel_id=1, source_target_pairs={{0,4},{4,8},{8,12},{12,16},{16,20},{20,24},{24,28},{1,5},{5,9},{9,... | collective-permute-start | bytes 1179656 | tf_op jit(solution)/shard_map/while/body/eval_jaxpr/ppermute | solution.py:15
  348.3 13.6 %collective-permute-start = (f32[4,192,128]{2,1,0:T(8,128)S(1)}, f32[4,192,128]{2,1,0:T(8,128)S(1)}, u32[]{:S(2)}, u32[]{:S(2)}) collective-permute-start(f32[4,192,128]{2,1,0:T(8,128)S(1)} %get-tuple-element.456), channel_id=1, source_target_pairs={{4,0},{8,4},{12,8},{16,12},{20,16},{24,20},{28,24},{5,1},{9,5},{13... | collective-permute-start | bytes 1179656 | tf_op jit(solution)/shard_map/while/body/eval_jaxpr/ppermute | solution.py:18
  357.4 5.4 copy-start.2
  376.9 17.5 %collective-permute-start.3 = (f32[4,192,128]{2,1,0:T(8,128)S(1)}, f32[4,192,128]{2,1,0:T(8,128)S(1)}, u32[]{:S(2)}, u32[]{:S(2)}) collective-permute-start(f32[4,192,128]{2,1,0:T(8,128)S(1)} %get-tuple-element.469), channel_id=1, source_target_pairs={{0,4},{4,8},{8,12},{12,16},{16,20},{20,24},{24,28},{1,5},{5,9},{9,... | collective-permute-start | bytes 1179656 | tf_op jit(solution)/shard_map/while/body/eval_jaxpr/ppermute | solution.py:15
  385.8 13.6 %collective-permute-start.2 = (f32[4,192,128]{2,1,0:T(8,128)S(1)}, f32[4,192,128]{2,1,0:T(8,128)S(1)}, u32[]{:S(2)}, u32[]{:S(2)}) collective-permute-start(f32[4,192,128]{2,1,0:T(8,128)S(1)} %get-tuple-element.468), channel_id=1, source_target_pairs={{4,0},{8,4},{12,8},{16,12},{20,16},{24,20},{28,24},{5,1},{9,5},{13... | collective-permute-start | bytes 1179656 | tf_op jit(solution)/shard_map/while/body/eval_jaxpr/ppermute | solution.py:18
  394.6 5.7 copy-start.3
  404.6 3.8 copy-start.4
  411.0 17.3 %collective-permute-start.3 = (f32[4,192,128]{2,1,0:T(8,128)S(1)}, f32[4,192,128]{2,1,0:T(8,128)S(1)}, u32[]{:S(2)}, u32[]{:S(2)}) collective-permute-start(f32[4,192,128]{2,1,0:T(8,128)S(1)} %get-tuple-element.469), channel_id=1, source_target_pairs={{0,4},{4,8},{8,12},{12,16},{16,20},{20,24},{24,28},{1,5},{5,9},{9,... | collective-permute-start | bytes 1179656 | tf_op jit(solution)/shard_map/while/body/eval_jaxpr/ppermute | solution.py:15
  419.7 13.6 %collective-permute-start.2 = (f32[4,192,128]{2,1,0:T(8,128)S(1)}, f32[4,192,128]{2,1,0:T(8,128)S(1)}, u32[]{:S(2)}, u32[]{:S(2)}) collective-permute-start(f32[4,192,128]{2,1,0:T(8,128)S(1)} %get-tuple-element.468), channel_id=1, source_target_pairs={{4,0},{8,4},{12,8},{16,12},{20,16},{24,20},{28,24},{5,1},{9,5},{13... | collective-permute-start | bytes 1179656 | tf_op jit(solution)/shard_map/while/body/eval_jaxpr/ppermute | solution.py:18
  428.5 5.7 copy-start.3
  445.0 17.3 %collective-permute-start.3 = (f32[4,192,128]{2,1,0:T(8,128)S(1)}, f32[4,192,128]{2,1,0:T(8,128)S(1)}, u32[]{:S(2)}, u32[]{:S(2)}) collective-permute-start(f32[4,192,128]{2,1,0:T(8,128)S(1)} %get-tuple-element.469), channel_id=1, source_target_pairs={{0,4},{4,8},{8,12},{12,16},{16,20},{20,24},{24,28},{1,5},{5,9},{9,... | collective-permute-start | bytes 1179656 | tf_op jit(solution)/shard_map/while/body/eval_jaxpr/ppermute | solution.py:15
  453.7 13.6 %collective-permute-start.2 = (f32[4,192,128]{2,1,0:T(8,128)S(1)}, f32[4,192,128]{2,1,0:T(8,128)S(1)}, u32[]{:S(2)}, u32[]{:S(2)}) collective-permute-start(f32[4,192,128]{2,1,0:T(8,128)S(1)} %get-tuple-element.468), channel_id=1, source_target_pairs={{4,0},{8,4},{12,8},{16,12},{20,16},{24,20},{28,24},{5,1},{9,5},{13... | collective-permute-start | bytes 1179656 | tf_op jit(solution)/shard_map/while/body/eval_jaxpr/ppermute | solution.py:18
  462.4 5.7 copy-start.3
  478.9 17.3 %collective-permute-start.3 = (f32[4,192,128]{2,1,0:T(8,128)S(1)}, f32[4,192,128]{2,1,0:T(8,128)S(1)}, u32[]{:S(2)}, u32[]{:S(2)}) collective-permute-start(f32[4,192,128]{2,1,0:T(8,128)S(1)} %get-tuple-element.469), channel_id=1, source_target_pairs={{0,4},{4,8},{8,12},{12,16},{16,20},{20,24},{24,28},{1,5},{5,9},{9,... | collective-permute-start | bytes 1179656 | tf_op jit(solution)/shard_map/while/body/eval_jaxpr/ppermute | solution.py:15
  487.6 13.6 %collective-permute-start.2 = (f32[4,192,128]{2,1,0:T(8,128)S(1)}, f32[4,192,128]{2,1,0:T(8,128)S(1)}, u32[]{:S(2)}, u32[]{:S(2)}) collective-permute-start(f32[4,192,128]{2,1,0:T(8,128)S(1)} %get-tuple-element.468), channel_id=1, source_target_pairs={{4,0},{8,4},{12,8},{16,12},{20,16},{24,20},{28,24},{5,1},{9,5},{13... | collective-permute-start | bytes 1179656 | tf_op jit(solution)/shard_map/while/body/eval_jaxpr/ppermute | solution.py:18
  496.4 5.7 copy-start.3
  512.8 17.3 %collective-permute-start.3 = (f32[4,192,128]{2,1,0:T(8,128)S(1)}, f32[4,192,128]{2,1,0:T(8,128)S(1)}, u32[]{:S(2)}, u32[]{:S(2)}) collective-permute-start(f32[4,192,128]{2,1,0:T(8,128)S(1)} %get-tuple-element.469), channel_id=1, source_target_pairs={{0,4},{4,8},{8,12},{12,16},{16,20},{20,24},{24,28},{1,5},{5,9},{9,... | collective-permute-start | bytes 1179656 | tf_op jit(solution)/shard_map/while/body/eval_jaxpr/ppermute | solution.py:15
  521.6 13.6 %collective-permute-start.2 = (f32[4,192,128]{2,1,0:T(8,128)S(1)}, f32[4,192,128]{2,1,0:T(8,128)S(1)}, u32[]{:S(2)}, u32[]{:S(2)}) collective-permute-start(f32[4,192,128]{2,1,0:T(8,128)S(1)} %get-tuple-element.468), channel_id=1, source_target_pairs={{4,0},{8,4},{12,8},{16,12},{20,16},{24,20},{28,24},{5,1},{9,5},{13... | collective-permute-start | bytes 1179656 | tf_op jit(solution)/shard_map/while/body/eval_jaxpr/ppermute | solution.py:18
  530.3 5.7 copy-start.3
  546.8 17.3 %collective-permute-start.3 = (f32[4,192,128]{2,1,0:T(8,128)S(1)}, f32[4,192,128]{2,1,0:T(8,128)S(1)}, u32[]{:S(2)}, u32[]{:S(2)}) collective-permute-start(f32[4,192,128]{2,1,0:T(8,128)S(1)} %get-tuple-element.469), channel_id=1, source_target_pairs={{0,4},{4,8},{8,12},{12,16},{16,20},{20,24},{24,28},{1,5},{5,9},{9,... | collective-permute-start | bytes 1179656 | tf_op jit(solution)/shard_map/while/body/eval_jaxpr/ppermute | solution.py:15
  555.5 13.6 %collective-permute-start.2 = (f32[4,192,128]{2,1,0:T(8,128)S(1)}, f32[4,192,128]{2,1,0:T(8,128)S(1)}, u32[]{:S(2)}, u32[]{:S(2)}) collective-permute-start(f32[4,192,128]{2,1,0:T(8,128)S(1)} %get-tuple-element.468), channel_id=1, source_target_pairs={{4,0},{8,4},{12,8},{16,12},{20,16},{24,20},{28,24},{5,1},{9,5},{13... | collective-permute-start | bytes 1179656 | tf_op jit(solution)/shard_map/while/body/eval_jaxpr/ppermute | solution.py:18
  564.3 5.7 copy-start.3
  574.2 3.8 copy-start.4
  580.7 17.3 %collective-permute-start.3 = (f32[4,192,128]{2,1,0:T(8,128)S(1)}, f32[4,192,128]{2,1,0:T(8,128)S(1)}, u32[]{:S(2)}, u32[]{:S(2)}) collective-permute-start(f32[4,192,128]{2,1,0:T(8,128)S(1)} %get-tuple-element.469), channel_id=1, source_target_pairs={{0,4},{4,8},{8,12},{12,16},{16,20},{20,24},{24,28},{1,5},{5,9},{9,... | collective-permute-start | bytes 1179656 | tf_op jit(solution)/shard_map/while/body/eval_jaxpr/ppermute | solution.py:15
  589.4 13.6 %collective-permute-start.2 = (f32[4,192,128]{2,1,0:T(8,128)S(1)}, f32[4,192,128]{2,1,0:T(8,128)S(1)}, u32[]{:S(2)}, u32[]{:S(2)}) collective-permute-start(f32[4,192,128]{2,1,0:T(8,128)S(1)} %get-tuple-element.468), channel_id=1, source_target_pairs={{4,0},{8,4},{12,8},{16,12},{20,16},{24,20},{28,24},{5,1},{9,5},{13... | collective-permute-start | bytes 1179656 | tf_op jit(solution)/shard_map/while/body/eval_jaxpr/ppermute | solution.py:18
  598.2 5.7 copy-start.3
  614.7 17.3 %collective-permute-start.3 = (f32[4,192,128]{2,1,0:T(8,128)S(1)}, f32[4,192,128]{2,1,0:T(8,128)S(1)}, u32[]{:S(2)}, u32[]{:S(2)}) collective-permute-start(f32[4,192,128]{2,1,0:T(8,128)S(1)} %get-tuple-element.469), channel_id=1, source_target_pairs={{0,4},{4,8},{8,12},{12,16},{16,20},{20,24},{24,28},{1,5},{5,9},{9,... | collective-permute-start | bytes 1179656 | tf_op jit(solution)/shard_map/while/body/eval_jaxpr/ppermute | solution.py:15
  623.4 13.6 %collective-permute-start.2 = (f32[4,192,128]{2,1,0:T(8,128)S(1)}, f32[4,192,128]{2,1,0:T(8,128)S(1)}, u32[]{:S(2)}, u32[]{:S(2)}) collective-permute-start(f32[4,192,128]{2,1,0:T(8,128)S(1)} %get-tuple-element.468), channel_id=1, source_target_pairs={{4,0},{8,4},{12,8},{16,12},{20,16},{24,20},{28,24},{5,1},{9,5},{13... | collective-permute-start | bytes 1179656 | tf_op jit(solution)/shard_map/while/body/eval_jaxpr/ppermute | solution.py:18
  632.1 5.7 copy-start.3
  648.6 17.3 %collective-permute-start.3 = (f32[4,192,128]{2,1,0:T(8,128)S(1)}, f32[4,192,128]{2,1,0:T(8,128)S(1)}, u32[]{:S(2)}, u32[]{:S(2)}) collective-permute-start(f32[4,192,128]{2,1,0:T(8,128)S(1)} %get-tuple-element.469), channel_id=1, source_target_pairs={{0,4},{4,8},{8,12},{12,16},{16,20},{20,24},{24,28},{1,5},{5,9},{9,... | collective-permute-start | bytes 1179656 | tf_op jit(solution)/shard_map/while/body/eval_jaxpr/ppermute | solution.py:15
  657.3 13.6 %collective-permute-start.2 = (f32[4,192,128]{2,1,0:T(8,128)S(1)}, f32[4,192,128]{2,1,0:T(8,128)S(1)}, u32[]{:S(2)}, u32[]{:S(2)}) collective-permute-start(f32[4,192,128]{2,1,0:T(8,128)S(1)} %get-tuple-element.468), channel_id=1, source_target_pairs={{4,0},{8,4},{12,8},{16,12},{20,16},{24,20},{28,24},{5,1},{9,5},{13... | collective-permute-start | bytes 1179656 | tf_op jit(solution)/shard_map/while/body/eval_jaxpr/ppermute | solution.py:18
  666.1 5.7 copy-start.3
  682.5 17.3 %collective-permute-start.3 = (f32[4,192,128]{2,1,0:T(8,128)S(1)}, f32[4,192,128]{2,1,0:T(8,128)S(1)}, u32[]{:S(2)}, u32[]{:S(2)}) collective-permute-start(f32[4,192,128]{2,1,0:T(8,128)S(1)} %get-tuple-element.469), channel_id=1, source_target_pairs={{0,4},{4,8},{8,12},{12,16},{16,20},{20,24},{24,28},{1,5},{5,9},{9,... | collective-permute-start | bytes 1179656 | tf_op jit(solution)/shard_map/while/body/eval_jaxpr/ppermute | solution.py:15
  691.2 13.6 %collective-permute-start.2 = (f32[4,192,128]{2,1,0:T(8,128)S(1)}, f32[4,192,128]{2,1,0:T(8,128)S(1)}, u32[]{:S(2)}, u32[]{:S(2)}) collective-permute-start(f32[4,192,128]{2,1,0:T(8,128)S(1)} %get-tuple-element.468), channel_id=1, source_target_pairs={{4,0},{8,4},{12,8},{16,12},{20,16},{24,20},{28,24},{5,1},{9,5},{13... | collective-permute-start | bytes 1179656 | tf_op jit(solution)/shard_map/while/body/eval_jaxpr/ppermute | solution.py:18
  700.0 5.7 copy-start.3
  (34 other events, 85.2 us)
Sparse Core Ops, SparseCore 0:
  716.6 28.6 reduce-scatter.1
where the time goes:
time: 760 us; the launch traced here: 754 us
  waiting for transfers between devices  239 us (31%)
  starting transfers between devices  201 us (26%)
  other arithmetic  199 us (26%)
  local copies, waits for them, and re-layouts  98.3 us (13%)
  between operations  14.1 us (2%)
    ppermute x20, starting transfers between devices, with_halo(): lax.ppermute(lax.slice_in_dim(block, block.shape[dim] - width, None, axis...  162 us
    ppermute x20, waiting for transfers between devices, with_halo(): lax.ppermute(lax.slice_in_dim(block, block.shape[dim] - width, None, axis...  131 us
    ppermute x20, waiting for transfers between devices, with_halo(): lax.ppermute(lax.slice_in_dim(block, 0, width, axis=dim), axis, backward)  79.1 us
    ppermute x20, starting transfers between devices, with_halo(): lax.ppermute(lax.slice_in_dim(block, 0, width, axis=dim), axis, backward)  38.9 us
    scatter-add x10, other arithmetic, backward(): earlier.reshape(-1).at[receiver_cells].add(residual).reshape(velocity.shape)  37.4 us
    while x180, local copies, waits for them, and re-layouts  33 us
    add x10, other arithmetic, backward(): 2.0 * following - furthest + courant_sq * laplace(edge_layers(following))  32.8 us
    add x10, other arithmetic, forward(): latest = 2.0 * current - former + courant_sq * laplace(edge_layers(current))  32.7 us
  transfers between devices with their start and end apart: 41, of which 38 were waited for; matrix products, arithmetic and copies ran while one was open for 4% of the time, Pallas kernels for 0%

commit v1 on v0

v1 whole, which is shorter than its diff:
```python
import jax
import jax.numpy as jnp
from jax import lax
from jax.experimental import pallas as pl
from jax.experimental.pallas import tpu as pltpu
from jax.sharding import PartitionSpec as P

TAPS = (-205.0 / 72.0, 8.0 / 5.0, -1.0 / 5.0, 8.0 / 315.0, -1.0 / 560.0)
COURANT = 0.09
MESH = pl.DeviceIdType.MESH
PAD = 8
H = 4
TROWS = 24
CHUNK = 32


def scatter_kernel(enc, senc, vals, svals, s_out, o_out, m_out, table):
    steps, lx, ly, lz = s_out.shape
    lines = lx * ly
    lane = lax.broadcasted_iota(jnp.int32, (8, lz), 1)

    def clear(i, _):
        table[pl.ds(pl.multiple_of(i * 64, 8), 64), :] = jnp.zeros((64, lz), jnp.float32)
        return 0

    lax.fori_loop(0, table.shape[0] // 64, clear, 0)

    def place(cells, values, first, tiles):
        loaded = [values[8 * k : 8 * k + 8, first : first + 128] for k in range(2)]

        def one(j, _):
            cell = cells[first + j]
            line = lax.shift_right_logical(cell, 7)
            z = cell & 127
            shift = (z - j) & 127
            here = lane == z
            base = pl.multiple_of(line * TROWS, 8)
            for value, tile in zip(loaded, tiles):
                at = pl.ds(pl.multiple_of(base + 8 * tile, 8), 8)
                table[at, :] = table[at, :] + jnp.where(here, pltpu.roll(value, shift, 1), 0.0)
            return 0

        lax.fori_loop(0, 128, one, 0, unroll=8)

    for first in range(0, enc.shape[0], 128):
        place(enc, vals, first, (0, 1))
    for first in range(0, senc.shape[0], 128):
        place(senc, svals, first, (2, 1))

    def spread(xi, _):
        for y0 in range(0, ly, 8):
            base = (xi * ly + y0) * TROWS
            for t in range(steps):
                o_out[t, xi, y0 : y0 + 8, :] = table[pl.ds(base + t, 8, stride=TROWS), :]
                row = 16 + t if t < 8 else 3 + t
                s_out[t, xi, y0 : y0 + 8, :] = table[pl.ds(base + row, 8, stride=TROWS), :]
            m_out[xi, y0 : y0 + 8, :] = table[pl.ds(base + 10, 8, stride=TROWS), :]
        return 0

    lax.fori_loop(0, lx, spread, 0)


def wave_kernel(
    vel, now, prev, adj, adjp, s_hbm, o_hbm, m_hbm, out,
    u, c2, velb, s_v, o_v, m_v, img, pair, red, got,
    halo_send, halo_recv, init_send, init_recv, loc, red_send, red_recv,
):
    cx, ny, nz = vel.shape
    lx, ly = 2 * cx, ny // 2
    steps = s_hbm.shape[0]
    n_space = lax.axis_size("space")
    i = lax.axis_index("space")
    s = lax.axis_index("shot")
    a, b = i // 2, i % 2
    x, core = s // 2, s % 2
    has_low = a > 0
    has_high = a < n_space // 2 - 1
    other_i = i + 1 - 2 * b
    other_s = s + 1 - 2 * core
    cross_s = s + 2 - 4 * x
    top = 2 * steps + 3

    def zero_low(l, _):
        u[l, 0:H, PAD : PAD + ly, :] = jnp.zeros((H, ly, nz), jnp.float32)
        return 0

    def zero_high(l, _):
        u[l, H + lx : lx + 2 * H, PAD : PAD + ly, :] = jnp.zeros((H, ly, nz), jnp.float32)
        return 0

    def zero_left(l, _):
        u[l, H : H + lx, 0:PAD, :] = jnp.zeros((lx, PAD, nz), jnp.float32)
        return 0

    def zero_right(l, _):
        u[l, H : H + lx, PAD + ly : 2 * PAD + ly, :] = jnp.zeros((lx, PAD, nz), jnp.float32)
        return 0

    @pl.when(jnp.logical_not(has_low))
    def _():
        lax.fori_loop(0, top, zero_low, 0)

    @pl.when(jnp.logical_not(has_high))
    def _():
        lax.fori_loop(0, top, zero_high, 0)

    @pl.when(b == 0)
    def _():
        lax.fori_loop(0, top, zero_left, 0)

    @pl.when(b == 1)
    def _():
        lax.fori_loop(0, top, zero_right, 0)

    level_of = (1, None, 0, steps + 3, steps + 2)
    sources = (now, vel, prev, adj, adjp)
    mine = pl.ds(pl.multiple_of(ly * b, 8), ly)
    theirs = pl.ds(pl.multiple_of(ly * (1 - b), 8), ly)

    def landing(k, half):
        if level_of[k] is None:
            return c2.at[pl.ds(cx * half, cx)]
        return u.at[level_of[k], pl.ds(H + cx * half, cx), PAD : PAD + ly, :]

    def view(k, rows):
        if k == 1:
            return sources[k].at[:, rows, :]
        return sources[k].at[0, :, rows, :]

    def local_copy(k):
        return pltpu.make_async_copy(view(k, mine), landing(k, b), loc.at[k])

    def partner_copy(k):
        return pltpu.make_async_remote_copy(
            src_ref=view(k, theirs), dst_ref=landing(k, b),
            send_sem=init_send.at[k], recv_sem=init_recv.at[k],
            device_id=(other_i, s), device_id_type=MESH,
        )

    extra = [
        pltpu.make_async_copy(s_hbm, s_v, loc.at[5]),
        pltpu.make_async_copy(m_hbm, m_v, loc.at[6]),
        pltpu.make_async_copy(
            vel.at[:, pl.ds(pl.multiple_of(velb.shape[1] * s, 8), velb.shape[1]), :], velb, loc.at[7]
        ),
        pltpu.make_async_copy(o_hbm, o_v, loc.at[8]),
    ]

    for k in range(5):
        local_copy(k).start()
    for copy in extra:
        copy.start()

    barrier = pltpu.get_barrier_semaphore()
    for target in ((other_i, s), (i, other_s), (i, cross_s), (other_i, cross_s)):
        pl.semaphore_signal(barrier, inc=1, device_id=target, device_id_type=MESH)

    @pl.when(has_low)
    def _():
        pl.semaphore_signal(barrier, inc=1, device_id=(i - 2, s), device_id_type=MESH)

    @pl.when(has_high)
    def _():
        pl.semaphore_signal(barrier, inc=1, device_id=(i + 2, s), device_id_type=MESH)

    pl.semaphore_wait(barrier, 4 + has_low.astype(jnp.int32) + has_high.astype(jnp.int32))

    for k in range(5):
        partner_copy(k).start()

    def send_up(l):
        return pltpu.make_async_remote_copy(
            src_ref=u.at[l, lx : lx + H, PAD : PAD + ly, :],
            dst_ref=u.at[l, 0:H, PAD : PAD + ly, :],
            send_sem=halo_send.at[l, 0], recv_sem=halo_recv.at[l, 0],
            device_id=(i + 2, s), device_id_type=MESH,
        )

    def send_down(l):
        return pltpu.make_async_remote_copy(
            src_ref=u.at[l, H : 2 * H, PAD : PAD + ly, :],
            dst_ref=u.at[l, lx + H : lx + 2 * H, PAD : PAD + ly, :],
            send_sem=halo_send.at[l, 1], recv_sem=halo_recv.at[l, 1],
            device_id=(i - 2, s), device_id_type=MESH,
        )

    def send_side(l):
        return pltpu.make_async_remote_copy(
            src_ref=u.at[l, H : H + lx, pl.ds(pl.multiple_of(ly - (ly - PAD) * b, 8), PAD), :],
            dst_ref=u.at[l, H : H + lx, pl.ds(pl.multiple_of((ly + PAD) * b, 8), PAD), :],
            send_sem=halo_send.at[l, 2], recv_sem=halo_recv.at[l, 2],
            device_id=(other_i, s), device_id_type=MESH,
        )

    def start_x(l):
        @pl.when(has_high)
        def _():
            send_up(l).start()

        @pl.when(has_low)
        def _():
            send_down(l).start()

    def wait_halos(l):
        send_side(l).wait()

        @pl.when(has_low)
        def _():
            send_up(l).wait_recv()
            send_down(l).wait_send()

        @pl.when(has_high)
        def _():
            send_down(l).wait_recv()
            send_up(l).wait_send()

    def settle(k):
        local_copy(k).wait()
        partner_copy(k).wait()

    lane = lax.broadcasted_iota(jnp.int32, (CHUNK, nz), 1)

    def laplace(l, xi, r0):
        rows = lambda d: slice(PAD + r0 + d, PAD + r0 + d + CHUNK)
        centre = u[l, H + xi, rows(0), :]
        result = 3.0 * TAPS[0] * centre
        for k in range(1, H + 1):
            beside = u[l, H + xi + k, rows(0), :] + u[l, H + xi - k, rows(0), :]
            beside = beside + u[l, H + xi, rows(k), :] + u[l, H + xi, rows(-k), :]
            beside = beside + jnp.where(lane < nz - k, pltpu.roll(centre, nz - k, 1), 0.0)
            beside = beside + jnp.where(lane >= k, pltpu.roll(centre, k, 1), 0.0)
            result = result + TAPS[k] * beside
        return centre, result

    def sweep(first, last, body):
        def layer(xi, _):
            for r0 in range(0, ly, CHUNK):
                body(xi, r0)
            return 0

        lax.fori_loop(first, last, layer, 0)

    settle(0)
    start_x(1)
    send_side(1).start()

    settle(1)

    def square(xi, r0):
        value = COURANT * c2[xi, r0 : r0 + CHUNK, :]
        c2[xi, r0 : r0 + CHUNK, :] = value * value
        img[xi, r0 : r0 + CHUNK, :] = jnp.zeros((CHUNK, nz), jnp.float32)

    sweep(0, lx, square)
    settle(2)
    for copy in extra:
        copy.wait()

    def forward(t, _):
        cur = t + 1

        def cell(xi, r0):
            rows = slice(PAD + r0, PAD + r0 + CHUNK)
            inner = slice(r0, r0 + CHUNK)
            centre, lap = laplace(cur, xi, r0)
            fresh = 2.0 * centre - u[t, H + xi, rows, :] + c2[xi, inner, :] * lap
            u[t + 2, H + xi, rows, :] = fresh + s_v[t, xi, inner, :]

        wait_halos(cur)
        sweep(0, H, cell)
        sweep(lx - H, lx, cell)

        @pl.when(t < steps - 1)
        def _():
            start_x(cur + 1)

        sweep(H, lx - H, cell)

        @pl.when(t < steps - 1)
        def _():
            send_side(cur + 1).start()

        return 0

    lax.fori_loop(0, steps, forward, 0)

    settle(3)
    settle(4)
    start_x(steps + 3)
    send_side(steps + 3).start()

    def backward(k, _):
        t = steps - 1 - k
        cur = steps + 3 + k

        def cell(xi, r0):
            rows = slice(PAD + r0, PAD + r0 + CHUNK)
            inner = slice(r0, r0 + CHUNK)
            centre, lap = laplace(cur, xi, r0)
            fresh = 2.0 * centre - u[cur - 1, H + xi, rows, :] + c2[xi, inner, :] * lap
            later = u[t + 2, H + xi, rows, :]
            fresh = fresh + m_v[xi, inner, :] * (later - o_v[t, xi, inner, :])
            accel = later - 2.0 * u[t + 1, H + xi, rows, :] + u[t, H + xi, rows, :]
            img[xi, inner, :] = img[xi, inner, :] + fresh * accel

            @pl.when(k < steps - 1)
            def _():
                u[cur + 1, H + xi, rows, :] = fresh

        wait_halos(cur)
        sweep(0, H, cell)
        sweep(lx - H, lx, cell)

        @pl.when(k < steps - 1)
        def _():
            start_x(cur + 1)

        sweep(H, lx - H, cell)

        @pl.when(k < steps - 1)
        def _():
            send_side(cur + 1).start()

        return 0

    lax.fori_loop(0, steps, backward, 0)

    band = velb.shape[1]
    keep = pl.multiple_of(band * core, 8)
    give = pl.multiple_of(band * (1 - core), 8)
    swap = pltpu.make_async_remote_copy(
        src_ref=img.at[:, pl.ds(give, band), :], dst_ref=pair,
        send_sem=red_send.at[2], recv_sem=red_recv.at[2],
        device_id=(i, other_s), device_id_type=MESH,
    )
    swap.start()
    swap.wait()

    def add_pair(xi, _):
        red[xi] = img[xi, pl.ds(keep, band), :] + pair[xi]
        return 0

    lax.fori_loop(0, lx, add_pair, 0)

    def deliver(target):
        return pltpu.make_async_remote_copy(
            src_ref=red.at[pl.ds(cx * target, cx)], dst_ref=got.at[x],
            send_sem=red_send.at[target], recv_sem=red_recv.at[x],
            device_id=(2 * a + target, 2 * b + core), device_id_type=MESH,
        )

    def arrival(k):
        return pltpu.make_async_remote_copy(
            src_ref=red.at[0:cx], dst_ref=got.at[k],
            send_sem=red_send.at[k], recv_sem=red_recv.at[k],
            device_id=(other_i, s), device_id_type=MESH,
        )

    for target in range(2):
        own = jnp.logical_and(x == b, b == target)

        @pl.when(jnp.logical_not(own))
        def _():
            deliver(target).start()

        @pl.when(own)
        def _():
            got[target] = red[cx * target : cx * (target + 1)]

    for k in range(2):
        own = jnp.logical_and(x == b, x == k)

        @pl.when(jnp.logical_not(own))
        def _():
            arrival(k).wait_recv()
            deliver(k).wait_send()

    for xi in range(cx):
        v = velb[xi]
        out[xi] = (-2.0 / (v * v * v)) * (got[0, xi] + got[1, xi])


def per_device(
    velocity, wave_now, wave_prev, adjoint_now, adjoint_prev,
    source_cells, wavelet, receiver_cells, receiver_counts, observed,
):
    cx, ny, nz = velocity.shape
    lx, ly = 2 * cx, ny // 2
    lines = lx * ly
    steps = wavelet.shape[1]
    slots = receiver_cells.shape[0]
    count = lax.axis_size("space")
    i = lax.axis_index("space")
    a, b = i // 2, i % 2
    swap = [(j, j + 1 - 2 * (j % 2)) for j in range(count)]

    live = jnp.arange(slots, dtype=jnp.int32) < receiver_counts[0]
    own_cells = jnp.where(live, receiver_cells, -1)
    their_cells = lax.ppermute(own_cells, "space", swap)
    their_obs = lax.ppermute(observed[0], "space", swap)

    def code(cells, layer0):
        line = cells // nz
        xg = line // ny + layer0
        yl = line % ny - ly * b
        ok = (cells >= 0) & (xg >= 0) & (xg < lx) & (yl >= 0) & (yl < ly)
        return jnp.where(ok, (xg * ly + yl) * nz + cells % nz, lines * nz)

    enc = jnp.concatenate([code(own_cells, cx * b), code(their_cells, cx * (1 - b))])
    senc = code(source_cells[0], -lx * a)
    vals = jnp.concatenate([observed[0], their_obs], axis=1)
    ones = jnp.ones((1, 2 * slots), jnp.float32)
    vals = jnp.concatenate([vals, ones, jnp.zeros((5, 2 * slots), jnp.float32)], axis=0)
    w = wavelet[0]
    gap = jnp.zeros((3, w.shape[1]), jnp.float32)
    svals = jnp.concatenate([w[:8], gap, w[8:], gap], axis=0)

    smem = pl.BlockSpec(memory_space=pltpu.SMEM)
    vmem = pl.BlockSpec(memory_space=pltpu.VMEM)
    anyw = pl.BlockSpec(memory_space=pl.ANY)
    f32 = jnp.float32
    dense = jax.ShapeDtypeStruct((steps, lx, ly, nz), f32)
    field = jax.ShapeDtypeStruct((lx, ly, nz), f32)
    s_f, o_f, m_f = pl.pallas_call(
        scatter_kernel,
        out_shape=(dense, dense, field),
        in_specs=[smem, smem, vmem, vmem],
        out_specs=(vmem, vmem, vmem),
        scratch_shapes=[pltpu.VMEM(((lines + 8) * TROWS, nz), f32)],
        compiler_params=pltpu.CompilerParams(vmem_limit_bytes=48 * 2**20),
        name="scatter",
    )(enc, senc, vals, svals)

    levels = 2 * steps + 3
    band = ny // 4
    dma = pltpu.SemaphoreType.DMA
    return pl.pallas_call(
        wave_kernel,
        out_shape=jax.ShapeDtypeStruct((cx, band, nz), f32),
        in_specs=[anyw] * 8,
        out_specs=vmem,
        scratch_shapes=[
            pltpu.VMEM((levels, lx + 2 * H, ly + 2 * PAD, nz), f32),
            pltpu.VMEM((lx, ly, nz), f32),
            pltpu.VMEM((cx, band, nz), f32),
            pltpu.VMEM((steps, lx, ly, nz), f32),
            pltpu.VMEM((steps, lx, ly, nz), f32),
            pltpu.VMEM((lx, ly, nz), f32),
            pltpu.VMEM((lx, ly, nz), f32),
            pltpu.VMEM((lx, band, nz), f32),
            pltpu.VMEM((lx, band, nz), f32),
            pltpu.VMEM((2, cx, band, nz), f32),
            dma((levels, 3)),
            dma((levels, 3)),
            dma((5,)),
            dma((5,)),
            dma((9,)),
            dma((3,)),
            dma((3,)),
        ],
        compiler_params=pltpu.CompilerParams(
            collective_id=0, has_side_effects=True, vmem_limit_bytes=60 * 2**20
        ),
        name="waves",
    )(velocity, wave_now, wave_prev, adjoint_now, adjoint_prev, s_f, o_f, m_f)


def solution(mesh):
    in_specs = (
        P("space", None, None),
        P("shot", "space", None, None),
        P("shot", "space", None, None),
        P("shot", "space", None, None),
        P("shot", "space", None, None),
        P("shot", None),
        P("shot", None, None),
        P("space"),
        P("space"),
        P("shot", None, "space"),
    )
    out_specs = P("space", "shot", None)
    return jax.shard_map(
        per_device, mesh=mesh, in_specs=in_specs, out_specs=out_specs, check_vma=False
    )
```

time: 760 us -> 256 us (0.34)
  Pallas kernels: 0 us -> 246 us
  waiting for transfers between devices: 239 us -> 0.01 us
  starting transfers between devices: 201 us -> 2.08 us
  other arithmetic: 199 us -> 1.51 us
  local copies, waits for them, and re-layouts: 98.3 us -> 4.78 us
  between operations: 14.1 us -> 0.71 us
    pallas_call x0 -> x2, Pallas kernels: none -> 246 us  [the longest x1 217 us: per_device(): pl.pallas_call(wave_kernel, out_shape=jax.ShapeDtypeStruct((cx, band, nz)...]
    ppermute x40 -> x2, waiting for transfers between devices: 210 us -> 0.01 us  [the longest x1 0.01 us: per_device(): their_obs = lax.ppermute(observed[0], 'space', swap)]
    ppermute x40 -> x2, starting transfers between devices: 201 us -> 2.08 us  [the longest x1 2.01 us: per_device(): their_obs = lax.ppermute(observed[0], 'space', swap)]
    add x30 -> x0, other arithmetic: 81.8 us -> none  [the longest x10 32.8 us: backward(): 2.0 * following - furthest + courant_sq * laplace(edge_layers(following))]
    scatter-add x20 -> x0, other arithmetic: 54.7 us -> none  [the longest x10 37.4 us: backward(): earlier.reshape(-1).at[receiver_cells].add(residual).reshape(velocity.shape)]
    while x180 -> x0, local copies, waits for them, and re-layouts: 33 us -> none
    gather x10 -> x0, local copies, waits for them, and re-layouts: 31.4 us -> none  [forward(): latest.reshape(-1)[receiver_cells]]
    reduce_scatter x1 -> x0, waiting for transfers between devices: 28.8 us -> none  [per_device(): lax.psum_scatter(imaging, 'shot', scatter_dimension=1, tiled=True)]
  transfers between devices with their start and end apart: 41 -> 2, of which waited for: 38 -> 0; matrix products, arithmetic and copies ran while one was open for 4% -> 1% of each run, Pallas kernels for 0% -> 0%
where the time goes in v1:
time: 256 us; the launch traced here: 255 us
  Pallas kernels  246 us (96%)
  local copies, waits for them, and re-layouts  4.78 us (2%)
    pallas_call x1, Pallas kernels, per_device(): pl.pallas_call(wave_kernel, out_shape=jax.ShapeDtypeStruct((cx, band, nz)...  217 us
    pallas_call x1, Pallas kernels, per_device(): pl.pallas_call(scatter_kernel, out_shape=(dense, dense, field), in_specs=...  28.9 us
  transfers between devices with their start and end apart: 2, of which 0 were waited for; matrix products, arithmetic and copies ran while one was open for 1% of the time, Pallas kernels for 0%

profile of v1, /device:TPU:4, one launch (start us, length us, event | category | flops | bytes accessed | tf_op | source)
XLA Modules:
  0.0 255.5 jit_solution(8315365968084701282)
XLA Ops:
  0.7 0.7 fusion.2
  1.4 0.1 collective-permute-start
  1.4 0.7 copy.17
  2.2 2.0 collective-permute-start.1
  4.2 0.7 slice.14
  4.9 0.7 slice.12
  5.6 0.7 and_select_fusion.1.senc
  6.3 0.1 pad.6.clone
  6.3 0.1 pad.7.clone
  6.4 0.0 collective-permute-done
  6.5 0.0 collective-permute-done.1
  6.5 0.1 maximum_maximum_fusion.vals
  6.6 28.9 %scatter.1 = (f32[10,16,96,128]{3,2,1,0:T(8,128)}, f32[10,16,96,128]{3,2,1,0:T(8,128)}, f32[16,96,128]{2,1,0:T(8,128)S(1)}) custom-call(s32[1024]{0:T(1024)S(1)} %pad_add_fusion.enc, s32[128]{0:T(128)S(1)} %and_select_fusion.1.senc, f32[16,1024]{1,0:T(8,128)S(1)} %maximum_maximum_fusion.vals, f32[16,128]{1,0:T(8,128)S(1)} %pad_maximum_fusion.svals), custom_call_target="tpu_custom_call" | custom-call | tf_op jit(solution)/shard_map/scatter/pallas_call | solution.py:424
  35.4 0.0 copy-start
  35.4 0.9 copy-done
  36.3 217.5 %waves.1 = f32[8,48,128]{2,1,0:T(8,128)} custom-call(f32[8,192,128]{2,1,0:T(8,128)} %vel.1, f32[1,8,192,128]{3,2,1,0:T(8,128)} %now.1, f32[1,8,192,128]{3,2,1,0:T(8,128)} %prev.1, f32[1,8,192,128]{3,2,1,0:T(8,128)} %adj.1, f32[1,8,192,128]{3,2,1,0:T(8,128)} %adjp.1, f32[10,16,96,128]{3,2,1,0:T(8,128)} %get-tuple-element.8.s_hbm, ...), custom_call_target="tpu_custom_call" | custom-call | tf_op jit(solution)/shard_map/waves/pallas_call | solution.py:437
  253.8 1.6 copy.20
  (5 shorter events, 0.0 us)
Async XLA Ops:
  1.4 5.1 %collective-permute-start = (s32[512]{0:T(512)S(1)}, s32[512]{0:T(512)S(1)}, u32[]{:S(2)}, u32[]{:S(2)}) collective-permute-start(s32[512]{0:T(512)S(1)} %get-tuple-element.12), channel_id=1, source_target_pairs={{0,4},{4,0},{8,12},{12,8},{16,20},{20,16},{24,28},{28,24},{1,5},{5... | collective-permute-start | bytes 6152 | tf_op jit(solution)/shard_map/ppermute | solution.py:399
  2.2 4.3 %collective-permute-start.1 = (f32[10,512]{1,0:T(8,128)S(1)}, f32[10,512]{1,0:T(8,128)S(1)}, u32[]{:S(2)}, u32[]{:S(2)}) collective-permute-start(f32[10,512]{1,0:T(8,128)S(1)} %bitcast.26), channel_id=1, source_target_pairs={{0,4},{4,0},{8,12},{12,8},{16,20},{20,16},{24,28},{28,24},{1,5},{5... | collective-permute-start | bytes 61448 | tf_op jit(solution)/shard_map/ppermute | solution.py:400
  35.4 0.9 copy-start

commit v2 on v1

--- a/solution.py
+++ b/solution.py
@@ -1,3 +1,5 @@
+import functools
+
 import jax
 import jax.numpy as jnp
 from jax import lax
@@ -10,7 +12,7 @@
 MESH = pl.DeviceIdType.MESH
 PAD = 8
 H = 4
-TROWS = 24
+TROWS = 21
 CHUNK = 32
 
 
@@ -34,9 +36,9 @@
             z = cell & 127
             shift = (z - j) & 127
             here = lane == z
-            base = pl.multiple_of(line * TROWS, 8)
+            base = line * TROWS
             for value, tile in zip(loaded, tiles):
-                at = pl.ds(pl.multiple_of(base + 8 * tile, 8), 8)
+                at = pl.ds(base + 8 * tile, 8)
                 table[at, :] = table[at, :] + jnp.where(here, pltpu.roll(value, shift, 1), 0.0)
             return 0
 
@@ -45,14 +47,14 @@
     for first in range(0, enc.shape[0], 128):
         place(enc, vals, first, (0, 1))
     for first in range(0, senc.shape[0], 128):
-        place(senc, svals, first, (2, 1))
+        place(senc, svals, first, (1, 2))
 
     def spread(xi, _):
         for y0 in range(0, ly, 8):
             base = (xi * ly + y0) * TROWS
             for t in range(steps):
                 o_out[t, xi, y0 : y0 + 8, :] = table[pl.ds(base + t, 8, stride=TROWS), :]
-                row = 16 + t if t < 8 else 3 + t
+                row = 11 + t
                 s_out[t, xi, y0 : y0 + 8, :] = table[pl.ds(base + row, 8, stride=TROWS), :]
             m_out[xi, y0 : y0 + 8, :] = table[pl.ds(base + 10, 8, stride=TROWS), :]
         return 0
@@ -63,7 +65,7 @@
 def wave_kernel(
     vel, now, prev, adj, adjp, s_hbm, o_hbm, m_hbm, out,
     u, c2, velb, s_v, o_v, m_v, img, pair, red, got,
-    halo_send, halo_recv, init_send, init_recv, loc, red_send, red_recv,
+    halo_send, halo_recv, init_send, init_recv, adj_send, adj_recv, loc, red_send, red_recv,
 ):
     cx, ny, nz = vel.shape
     lx, ly = 2 * cx, ny // 2
@@ -137,6 +139,14 @@
             device_id=(other_i, s), device_id_type=MESH,
         )
 
+    def partner_layer(k, layer):
+        return pltpu.make_async_remote_copy(
+            src_ref=sources[k].at[0, layer, theirs, :],
+            dst_ref=u.at[level_of[k], H + cx * b + layer, PAD : PAD + ly, :],
+            send_sem=adj_send.at[k - 3, layer], recv_sem=adj_recv.at[k - 3, layer],
+            device_id=(other_i, s), device_id_type=MESH,
+        )
+
     extra = [
         pltpu.make_async_copy(s_hbm, s_v, loc.at[5]),
         pltpu.make_async_copy(m_hbm, m_v, loc.at[6]),
@@ -165,22 +175,26 @@
 
     pl.semaphore_wait(barrier, 4 + has_low.astype(jnp.int32) + has_high.astype(jnp.int32))
 
-    for k in range(5):
+    for k in range(3):
         partner_copy(k).start()
 
-    def send_up(l):
-        return pltpu.make_async_remote_copy(
-            src_ref=u.at[l, lx : lx + H, PAD : PAD + ly, :],
-            dst_ref=u.at[l, 0:H, PAD : PAD + ly, :],
-            send_sem=halo_send.at[l, 0], recv_sem=halo_recv.at[l, 0],
+    pieces = ly // CHUNK
+
+    def send_up(l, p):
+        rows = slice(PAD + CHUNK * p, PAD + CHUNK * (p + 1))
+        return pltpu.make_async_remote_copy(
+            src_ref=u.at[l, lx : lx + H, rows, :],
+            dst_ref=u.at[l, 0:H, rows, :],
+            send_sem=halo_send.at[l, p], recv_sem=halo_recv.at[l, p],
             device_id=(i + 2, s), device_id_type=MESH,
         )
 
-    def send_down(l):
-        return pltpu.make_async_remote_copy(
-            src_ref=u.at[l, H : 2 * H, PAD : PAD + ly, :],
-            dst_ref=u.at[l, lx + H : lx + 2 * H, PAD : PAD + ly, :],
-            send_sem=halo_send.at[l, 1], recv_sem=halo_recv.at[l, 1],
+    def send_down(l, p):
+        rows = slice(PAD + CHUNK * p, PAD + CHUNK * (p + 1))
+        return pltpu.make_async_remote_copy(
+            src_ref=u.at[l, H : 2 * H, rows, :],
+            dst_ref=u.at[l, lx + H : lx + 2 * H, rows, :],
+            send_sem=halo_send.at[l, pieces + p], recv_sem=halo_recv.at[l, pieces + p],
             device_id=(i - 2, s), device_id_type=MESH,
         )
 
@@ -188,31 +202,37 @@
         return pltpu.make_async_remote_copy(
             src_ref=u.at[l, H : H + lx, pl.ds(pl.multiple_of(ly - (ly - PAD) * b, 8), PAD), :],
             dst_ref=u.at[l, H : H + lx, pl.ds(pl.multiple_of((ly + PAD) * b, 8), PAD), :],
-            send_sem=halo_send.at[l, 2], recv_sem=halo_recv.at[l, 2],
+            send_sem=halo_send.at[l, 2 * pieces], recv_sem=halo_recv.at[l, 2 * pieces],
             device_id=(other_i, s), device_id_type=MESH,
         )
 
-    def start_x(l):
+    def start_down(l, p):
+        @pl.when(has_low)
+        def _():
+            send_down(l, p).start()
+
+    def start_up(l, p):
         @pl.when(has_high)
         def _():
-            send_up(l).start()
-
+            send_up(l, p).start()
+
+    def start_all(l, order):
+        send_side(l).start()
+        for p in order:
+            start_down(l, p)
+            start_up(l, p)
+
+    def wait_low(l, p):
         @pl.when(has_low)
         def _():
-            send_down(l).start()
-
-    def wait_halos(l):
-        send_side(l).wait()
-
-        @pl.when(has_low)
-        def _():
-            send_up(l).wait_recv()
-            send_down(l).wait_send()
-
+            send_up(l, p).wait_recv()
+            send_down(l, p).wait_send()
+
+    def wait_high(l, p):
         @pl.when(has_high)
         def _():
-            send_down(l).wait_recv()
-            send_up(l).wait_send()
+            send_down(l, p).wait_recv()
+            send_up(l, p).wait_send()
 
     def settle(k):
         local_copy(k).wait()
@@ -232,31 +252,44 @@
             result = result + TAPS[k] * beside
         return centre, result
 
-    def sweep(first, last, body):
+    def sweep(first, last, p, body):
         def layer(xi, _):
-            for r0 in range(0, ly, CHUNK):
-                body(xi, r0)
+            body(xi, CHUNK * p)
             return 0
 
-        lax.fori_loop(first, last, layer, 0)
-
-    settle(0)
-    start_x(1)
-    send_side(1).start()
-
-    settle(1)
+        lax.fori_loop(first, last, layer, 0, unroll=2)
+
+    def step(cur, more, order, cell):
+        for n, p in enumerate(order):
+            if n == 0:
+                send_side(cur).wait()
+            wait_low(cur, p)
+            sweep(0, H, p, cell)
+
+            @pl.when(more)
+            def _():
+                start_down(cur + 1, p)
+
+            wait_high(cur, p)
+            sweep(lx - H, lx, p, cell)
+
+            @pl.when(more)
+            def _():
+                start_up(cur + 1, p)
+
+            sweep(H, lx - H, p, cell)
+            if n == 0:
+
+                @pl.when(more)
+                def _():
+                    send_side(cur + 1).start()
 
     def square(xi, r0):
         value = COURANT * c2[xi, r0 : r0 + CHUNK, :]
         c2[xi, r0 : r0 + CHUNK, :] = value * value
         img[xi, r0 : r0 + CHUNK, :] = jnp.zeros((CHUNK, nz), jnp.float32)
 
-    sweep(0, lx, square)
-    settle(2)
-    for copy in extra:
-        copy.wait()
-
-    def forward(t, _):
+    def forward(order, t, _):
         cur = t + 1
 
         def cell(xi, r0):
@@ -266,30 +299,28 @@
             fresh = 2.0 * centre - u[t, H + xi, rows, :] + c2[xi, inner, :] * lap
             u[t + 2, H + xi, rows, :] = fresh + s_v[t, xi, inner, :]
 
-        wait_halos(cur)
-        sweep(0, H, cell)
-        sweep(lx - H, lx, cell)
-
-        @pl.when(t < steps - 1)
-        def _():
-            start_x(cur + 1)
-
-        sweep(H, lx - H, cell)
-
-        @pl.when(t < steps - 1)
-        def _():
-            send_side(cur + 1).start()
-
-        return 0
-
-    lax.fori_loop(0, steps, forward, 0)
-
-    settle(3)
-    settle(4)
-    start_x(steps + 3)
-    send_side(steps + 3).start()
-
-    def backward(k, _):
+        @pl.when(t < cx)
+        def _():
+            partner_layer(3, t).start()
+            partner_layer(4, t).start()
+
+        step(cur, t < steps - 1, order, cell)
+
+        @pl.when(t == steps - 2)
+        def _():
+            for k in (3, 4):
+                local_copy(k).wait()
+
+                def arrive(layer, _):
+                    partner_layer(k, layer).wait()
+                    return 0
+
+                lax.fori_loop(0, cx, arrive, 0)
+            start_all(steps + 3, order)
+
+        return 0
+
+    def backward(order, k, _):
         t = steps - 1 - k
         cur = steps + 3 + k
 
@@ -302,28 +333,30 @@
             fresh = fresh + m_v[xi, inner, :] * (later - o_v[t, xi, inner, :])
             accel = later - 2.0 * u[t + 1, H + xi, rows, :] + u[t, H + xi, rows, :]
             img[xi, inner, :] = img[xi, inner, :] + fresh * accel
-
-            @pl.when(k < steps - 1)
-            def _():
-                u[cur + 1, H + xi, rows, :] = fresh
-
-        wait_halos(cur)
-        sweep(0, H, cell)
-        sweep(lx - H, lx, cell)
-
-        @pl.when(k < steps - 1)
-        def _():
-            start_x(cur + 1)
-
-        sweep(H, lx - H, cell)
-
-        @pl.when(k < steps - 1)
-        def _():
-            send_side(cur + 1).start()
-
-        return 0
-
-    lax.fori_loop(0, steps, backward, 0)
+            u[cur + 1, H + xi, rows, :] = fresh
+
+        step(cur, k < steps - 1, order, cell)
+        return 0
+
+    def both(order):
+        settle(0)
+        start_all(1, order)
+        settle(1)
+        for p in order:
+            sweep(0, lx, p, square)
+        settle(2)
+        for copy in extra:
+            copy.wait()
+        lax.fori_loop(0, steps, functools.partial(forward, order), 0)
+        lax.fori_loop(0, steps, functools.partial(backward, order), 0)
+
+    @pl.when(b == 0)
+    def _():
+        both(tuple(range(pieces - 1, -1, -1)))
+
+    @pl.when(b == 1)
+    def _():
+        both(tuple(range(pieces)))
 
     band = velb.shape[1]
     keep = pl.multiple_of(band * core, 8)
@@ -413,7 +446,7 @@
     vals = jnp.concatenate([vals, ones, jnp.zeros((5, 2 * slots), jnp.float32)], axis=0)
     w = wavelet[0]
     gap = jnp.zeros((3, w.shape[1]), jnp.float32)
-    svals = jnp.concatenate([w[:8], gap, w[8:], gap], axis=0)
+    svals = jnp.concatenate([gap, w, gap], axis=0)
 
     smem = pl.BlockSpec(memory_space=pltpu.SMEM)
     vmem = pl.BlockSpec(memory_space=pltpu.VMEM)
@@ -426,12 +459,12 @@
         out_shape=(dense, dense, field),
         in_specs=[smem, smem, vmem, vmem],
         out_specs=(vmem, vmem, vmem),
-        scratch_shapes=[pltpu.VMEM(((lines + 8) * TROWS, nz), f32)],
+        scratch_shapes=[pltpu.VMEM(((lines + 64) * TROWS, nz), f32)],
         compiler_params=pltpu.CompilerParams(vmem_limit_bytes=48 * 2**20),
         name="scatter",
     )(enc, senc, vals, svals)
 
-    levels = 2 * steps + 3
+    levels = 2 * steps + 4
     band = ny // 4
     dma = pltpu.SemaphoreType.DMA
     return pl.pallas_call(
@@ -450,10 +483,12 @@
             pltpu.VMEM((lx, band, nz), f32),
             pltpu.VMEM((lx, band, nz), f32),
             pltpu.VMEM((2, cx, band, nz), f32),
-            dma((levels, 3)),
-            dma((levels, 3)),
-            dma((5,)),
-            dma((5,)),
+            dma((levels, 2 * (ly // CHUNK) + 1)),
+            dma((levels, 2 * (ly // CHUNK) + 1)),
+            dma((3,)),
+            dma((3,)),
+            dma((2, cx)),
+            dma((2, cx)),
             dma((9,)),
             dma((3,)),
             dma((3,)),

time: 256 us -> 175 us (0.68)
  Pallas kernels: 246 us -> 166 us
    pallas_call x1, Pallas kernels: 217 us -> 139 us  [per_device(): pl.pallas_call(wave_kernel, out_shape=jax.ShapeDtypeStruct((cx, band, nz)...]
  transfers between devices with their start and end apart: 2 -> 2, of which waited for: 0 -> 1; matrix products, arithmetic and copies ran while one was open for 1% -> 1% of each run, Pallas kernels for 0% -> 0%
where the time goes in v2:
time: 175 us
  Pallas kernels  166 us (95%)
  local copies, waits for them, and re-layouts  4.1 us (2%)
  starting transfers between devices  2.08 us (1%)
    pallas_call x1, Pallas kernels, per_device(): pl.pallas_call(wave_kernel, out_shape=jax.ShapeDtypeStruct((cx, band, nz)...  139 us
    pallas_call x1, Pallas kernels, per_device(): pl.pallas_call(scatter_kernel, out_shape=(dense, dense, field), in_specs=...  27.4 us
    unnamed x5, local copies, waits for them, and re-layouts  3.94 us
  transfers between devices with their start and end apart: 2, of which 1 were waited for; matrix products, arithmetic and copies ran while one was open for 1% of the time, Pallas kernels for 0%

profile of v2, /device:TPU:4, one launch (start us, length us, event | category | flops | bytes accessed | tf_op | source)
XLA Modules:
  0.0 174.7 jit_solution(475099277965664554)
XLA Ops:
  0.7 0.7 fusion.2
  1.4 0.1 collective-permute-start
  1.4 0.7 copy.15
  2.2 2.0 %collective-permute-start.1 = (f32[10,512]{1,0:T(8,128)S(1)}, f32[10,512]{1,0:T(8,128)S(1)}, u32[]{:S(2)}, u32[]{:S(2)}) collective-permute-start(f32[10,512]{1,0:T(8,128)S(1)} %bitcast.23), channel_id=1, source_target_pairs={{0,4},{4,0},{8,12},{12,8},{16,20},{20,16},{24,28},{28,24},{1,5},{5... | collective-permute-start | bytes 61448 | tf_op jit(solution)/shard_map/ppermute | solution.py:433
  4.2 0.7 copy.16
  4.9 0.7 and_select_fusion.1.senc
  5.6 0.1 pad.5.clone
  5.7 0.1 pad.6.clone
  5.7 0.0 collective-permute-done
  5.8 0.3 collective-permute-done.1
  6.1 0.1 maximum_maximum_fusion.vals
  6.2 27.4 %scatter.1 = (f32[10,16,96,128]{3,2,1,0:T(8,128)}, f32[10,16,96,128]{3,2,1,0:T(8,128)}, f32[16,96,128]{2,1,0:T(8,128)S(1)}) custom-call(s32[1024]{0:T(1024)S(1)} %pad_add_fusion.enc, s32[128]{0:T(128)S(1)} %and_select_fusion.1.senc, f32[16,1024]{1,0:T(8,128)S(1)} %maximum_maximum_fusion.vals, f32[16,128]{1,0:T(8,128)S(1)} %pad_maximum_fusion.svals), custom_call_target="tpu_custom_call" | custom-call | tf_op jit(solution)/shard_map/scatter/pallas_call | solution.py:457
  33.6 0.0 copy-start
  33.6 0.9 copy-done
  34.5 138.6 %waves.1 = f32[8,48,128]{2,1,0:T(8,128)} custom-call(f32[8,192,128]{2,1,0:T(8,128)} %vel.1, f32[1,8,192,128]{3,2,1,0:T(8,128)} %now.1, f32[1,8,192,128]{3,2,1,0:T(8,128)} %prev.1, f32[1,8,192,128]{3,2,1,0:T(8,128)} %adj.1, f32[1,8,192,128]{3,2,1,0:T(8,128)} %adjp.1, f32[10,16,96,128]{3,2,1,0:T(8,128)} %get-tuple-element.8.s_hbm, ...), custom_call_target="tpu_custom_call" | custom-call | tf_op jit(solution)/shard_map/waves/pallas_call | solution.py:470
  173.1 1.6 copy.19
  (5 shorter events, 0.0 us)
Async XLA Ops:
  1.4 4.4 %collective-permute-start = (s32[512]{0:T(512)S(1)}, s32[512]{0:T(512)S(1)}, u32[]{:S(2)}, u32[]{:S(2)}) collective-permute-start(s32[512]{0:T(512)S(1)} %get-tuple-element.12), channel_id=1, source_target_pairs={{0,4},{4,0},{8,12},{12,8},{16,20},{20,16},{24,28},{28,24},{1,5},{5... | collective-permute-start | bytes 6152 | tf_op jit(solution)/shard_map/ppermute | solution.py:432
  2.2 3.9 %collective-permute-start.1 = (f32[10,512]{1,0:T(8,128)S(1)}, f32[10,512]{1,0:T(8,128)S(1)}, u32[]{:S(2)}, u32[]{:S(2)}) collective-permute-start(f32[10,512]{1,0:T(8,128)S(1)} %bitcast.23), channel_id=1, source_target_pairs={{0,4},{4,0},{8,12},{12,8},{16,20},{20,16},{24,28},{28,24},{1,5},{5... | collective-permute-start | bytes 61448 | tf_op jit(solution)/shard_map/ppermute | solution.py:433
  33.6 0.9 copy-start

commit v3 on v2

--- a/solution.py
+++ b/solution.py
@@ -16,56 +16,82 @@
 CHUNK = 32
 
 
-def scatter_kernel(enc, senc, vals, svals, s_out, o_out, m_out, table):
-    steps, lx, ly, lz = s_out.shape
-    lines = lx * ly
+def scatter_kernel(
+    enc, senc, vals, svals, s_out, o_out, m_out, low, high, s_v, o_v, m_v, sems
+):
+    steps, lx, ly, lz = s_v.shape
+    half = lx // 2
+    slots = enc.shape[1]
     lane = lax.broadcasted_iota(jnp.int32, (8, lz), 1)
 
     def clear(i, _):
-        table[pl.ds(pl.multiple_of(i * 64, 8), 64), :] = jnp.zeros((64, lz), jnp.float32)
-        return 0
-
-    lax.fori_loop(0, table.shape[0] // 64, clear, 0)
+        at = pl.ds(pl.multiple_of(i * 64, 8), 64)
+        low[at, :] = jnp.zeros((64, lz), jnp.float32)
+        high[at, :] = jnp.zeros((64, lz), jnp.float32)
+        return 0
+
+    lax.fori_loop(0, low.shape[0] // 64, clear, 0)
 
     def place(cells, values, first, tiles):
-        loaded = [values[8 * k : 8 * k + 8, first : first + 128] for k in range(2)]
-
         def one(j, _):
-            cell = cells[first + j]
-            line = lax.shift_right_logical(cell, 7)
-            z = cell & 127
-            shift = (z - j) & 127
-            here = lane == z
-            base = line * TROWS
-            for value, tile in zip(loaded, tiles):
-                at = pl.ds(base + 8 * tile, 8)
-                table[at, :] = table[at, :] + jnp.where(here, pltpu.roll(value, shift, 1), 0.0)
+            places = []
+            for h, table in enumerate((low, high)):
+                cell = cells[h, first + j]
+                line = lax.shift_right_logical(cell, 7)
+                z = cell & 127
+                shift = (z - j) & 127
+                here = lane == z
+                for k, tile in enumerate(tiles):
+                    value = values[h % values.shape[0], 8 * k : 8 * k + 8, first : first + 128]
+                    at = pl.ds(line * TROWS + 8 * tile, 8)
+                    added = jnp.where(here, pltpu.roll(value, shift, 1), 0.0)
+                    places.append((table, at, table[at, :] + added))
+            for table, at, value in places:
+                table[at, :] = value
             return 0
 
         lax.fori_loop(0, 128, one, 0, unroll=8)
 
-    for first in range(0, enc.shape[0], 128):
+    for first in range(0, slots, 128):
         place(enc, vals, first, (0, 1))
-    for first in range(0, senc.shape[0], 128):
+    for first in range(0, senc.shape[1], 128):
         place(senc, svals, first, (1, 2))
 
-    def spread(xi, _):
-        for y0 in range(0, ly, 8):
-            base = (xi * ly + y0) * TROWS
-            for t in range(steps):
-                o_out[t, xi, y0 : y0 + 8, :] = table[pl.ds(base + t, 8, stride=TROWS), :]
-                row = 11 + t
-                s_out[t, xi, y0 : y0 + 8, :] = table[pl.ds(base + row, 8, stride=TROWS), :]
-            m_out[xi, y0 : y0 + 8, :] = table[pl.ds(base + 10, 8, stride=TROWS), :]
-        return 0
-
-    lax.fori_loop(0, lx, spread, 0)
+    def copies(xi):
+        return (
+            pltpu.make_async_copy(s_v.at[:, xi], s_out.at[:, xi], sems.at[0, xi]),
+            pltpu.make_async_copy(o_v.at[:, xi], o_out.at[:, xi], sems.at[1, xi]),
+            pltpu.make_async_copy(m_v.at[xi], m_out.at[xi], sems.at[2, xi]),
+        )
+
+    for h, table in enumerate((low, high)):
+
+        def spread(x0, _):
+            xi = x0 + half * h
+            for y0 in range(0, ly, 8):
+                base = (x0 * ly + y0) * TROWS
+                for t in range(steps):
+                    o_v[t, xi, y0 : y0 + 8, :] = table[pl.ds(base + t, 8, stride=TROWS), :]
+                    s_v[t, xi, y0 : y0 + 8, :] = table[pl.ds(base + 11 + t, 8, stride=TROWS), :]
+                m_v[xi, y0 : y0 + 8, :] = table[pl.ds(base + 10, 8, stride=TROWS), :]
+            for copy in copies(xi):
+                copy.start()
+            return 0
+
+        lax.fori_loop(0, half, spread, 0)
+
+    def finish(xi, _):
+        for copy in copies(xi):
+            copy.wait()
+        return 0
+
+    lax.fori_loop(0, lx, finish, 0)
 
 
 def wave_kernel(
-    vel, now, prev, adj, adjp, s_hbm, o_hbm, m_hbm, out,
+    vel, now, prev, adj, adjp, far, same, cross, s_hbm, o_hbm, m_hbm, out,
     u, c2, velb, s_v, o_v, m_v, img, pair, red, got,
-    halo_send, halo_recv, init_send, init_recv, adj_send, adj_recv, loc, red_send, red_recv,
+    halo_send, halo_recv, adj_send, adj_recv, loc, s_sem, red_send, red_recv,
 ):
     cx, ny, nz = vel.shape
     lx, ly = 2 * cx, ny // 2
@@ -132,12 +158,19 @@
     def local_copy(k):
         return pltpu.make_async_copy(view(k, mine), landing(k, b), loc.at[k])
 
-    def partner_copy(k):
-        return pltpu.make_async_remote_copy(
-            src_ref=view(k, theirs), dst_ref=landing(k, b),
-            send_sem=init_send.at[k], recv_sem=init_recv.at[k],
-            device_id=(other_i, s), device_id_type=MESH,
-        )
+    def far_copy(k):
+        return pltpu.make_async_copy(far.at[k], landing(k, 1 - b), loc.at[8 + k])
+
+    def low_copy(first):
+        return pltpu.make_async_copy(first, u.at[1, 0:H, PAD : PAD + ly, :], loc.at[11])
+
+    def high_copy(first):
+        return pltpu.make_async_copy(
+            first, u.at[1, H + lx : lx + 2 * H, PAD : PAD + ly, :], loc.at[12]
+        )
+
+    def s_copy(k):
+        return pltpu.make_async_copy(s_hbm.at[k], s_v.at[k], s_sem.at[k])
 
     def partner_layer(k, layer):
         return pltpu.make_async_remote_copy(
@@ -148,15 +181,31 @@
         )
 
     extra = [
-        pltpu.make_async_copy(s_hbm, s_v, loc.at[5]),
-        pltpu.make_async_copy(m_hbm, m_v, loc.at[6]),
+        pltpu.make_async_copy(m_hbm, m_v, loc.at[5]),
         pltpu.make_async_copy(
-            vel.at[:, pl.ds(pl.multiple_of(velb.shape[1] * s, 8), velb.shape[1]), :], velb, loc.at[7]
+            vel.at[:, pl.ds(pl.multiple_of(velb.shape[1] * s, 8), velb.shape[1]), :], velb, loc.at[6]
         ),
-        pltpu.make_async_copy(o_hbm, o_v, loc.at[8]),
+        pltpu.make_async_copy(o_hbm, o_v, loc.at[7]),
     ]
 
-    for k in range(5):
+    def each_edge(call):
+        for parity, low, high in ((0, cross, same), (1, same, cross)):
+
+            @pl.when(jnp.logical_and(b == parity, has_low))
+            def _():
+                call(low_copy(low))
+
+            @pl.when(jnp.logical_and(b == parity, has_high))
+            def _():
+                call(high_copy(high))
+
+    for k in range(3):
+        local_copy(k).start()
+        far_copy(k).start()
+    each_edge(lambda copy: copy.start())
+    for k in range(steps):
+        s_copy(k).start()
+    for k in (3, 4):
         local_copy(k).start()
     for copy in extra:
         copy.start()
@@ -175,8 +224,6 @@
 
     pl.semaphore_wait(barrier, 4 + has_low.astype(jnp.int32) + has_high.astype(jnp.int32))
 
-    for k in range(3):
-        partner_copy(k).start()
 
     pieces = ly // CHUNK
 
@@ -222,21 +269,21 @@
             start_down(l, p)
             start_up(l, p)
 
-    def wait_low(l, p):
-        @pl.when(has_low)
+    def wait_low(l, p, arrives):
+        @pl.when(jnp.logical_and(has_low, arrives))
         def _():
             send_up(l, p).wait_recv()
             send_down(l, p).wait_send()
 
-    def wait_high(l, p):
-        @pl.when(has_high)
+    def wait_high(l, p, arrives):
+        @pl.when(jnp.logical_and(has_high, arrives))
         def _():
             send_down(l, p).wait_recv()
             send_up(l, p).wait_send()
 
     def settle(k):
         local_copy(k).wait()
-        partner_copy(k).wait()
+        far_copy(k).wait()
 
     lane = lax.broadcasted_iota(jnp.int32, (CHUNK, nz), 1)
 
@@ -259,18 +306,18 @@
 
         lax.fori_loop(first, last, layer, 0, unroll=2)
 
-    def step(cur, more, order, cell):
+    def step(cur, arrives, more, order, cell):
         for n, p in enumerate(order):
             if n == 0:
                 send_side(cur).wait()
-            wait_low(cur, p)
+            wait_low(cur, p, arrives)
             sweep(0, H, p, cell)
 
             @pl.when(more)
             def _():
                 start_down(cur + 1, p)
 
-            wait_high(cur, p)
+            wait_high(cur, p, arrives)
             sweep(lx - H, lx, p, cell)
 
             @pl.when(more)
@@ -304,7 +351,8 @@
             partner_layer(3, t).start()
             partner_layer(4, t).start()
 
-        step(cur, t < steps - 1, order, cell)
+        s_copy(t).wait()
+        step(cur, t > 0, t < steps - 1, order, cell)
 
         @pl.when(t == steps - 2)
         def _():
@@ -335,19 +383,20 @@
             img[xi, inner, :] = img[xi, inner, :] + fresh * accel
             u[cur + 1, H + xi, rows, :] = fresh
 
-        step(cur, k < steps - 1, order, cell)
+        step(cur, True, k < steps - 1, order, cell)
         return 0
 
     def both(order):
         settle(0)
-        start_all(1, order)
+        send_side(1).start()
         settle(1)
         for p in order:
             sweep(0, lx, p, square)
         settle(2)
+        each_edge(lambda copy: copy.wait())
+        lax.fori_loop(0, steps, functools.partial(forward, order), 0)
         for copy in extra:
             copy.wait()
-        lax.fori_loop(0, steps, functools.partial(forward, order), 0)
         lax.fori_loop(0, steps, functools.partial(backward, order), 0)
 
     @pl.when(b == 0)
@@ -432,21 +481,39 @@
     their_cells = lax.ppermute(own_cells, "space", swap)
     their_obs = lax.ppermute(observed[0], "space", swap)
 
-    def code(cells, layer0):
+    def rows_of(block, part):
+        return lax.dynamic_slice_in_dim(block, ly * part, ly, 1)
+
+    far = jnp.stack([rows_of(f, 1 - b) for f in (wave_now[0], velocity, wave_prev[0])])
+    far = lax.ppermute(far, "space", swap)
+    edge = lax.dynamic_slice_in_dim(wave_now[0], (cx - H) * b, H, 0)
+    beyond = [(j, j + 4 * (j % 2) - 2) for j in range(count)]
+    across = [(j, j + 2 * (j % 2) - 1) for j in range(count)]
+    within = lambda pairs: [(j, k) for j, k in pairs if 0 <= k < count]
+    same = lax.ppermute(rows_of(edge, b), "space", within(beyond))
+    cross = lax.ppermute(rows_of(edge, 1 - b), "space", within(across))
+
+    def code(cells, layer0, layers):
         line = cells // nz
         xg = line // ny + layer0
         yl = line % ny - ly * b
-        ok = (cells >= 0) & (xg >= 0) & (xg < lx) & (yl >= 0) & (yl < ly)
-        return jnp.where(ok, (xg * ly + yl) * nz + cells % nz, lines * nz)
-
-    enc = jnp.concatenate([code(own_cells, cx * b), code(their_cells, cx * (1 - b))])
-    senc = code(source_cells[0], -lx * a)
-    vals = jnp.concatenate([observed[0], their_obs], axis=1)
-    ones = jnp.ones((1, 2 * slots), jnp.float32)
-    vals = jnp.concatenate([vals, ones, jnp.zeros((5, 2 * slots), jnp.float32)], axis=0)
+        ok = (cells >= 0) & (xg >= 0) & (xg < layers) & (yl >= 0) & (yl < ly)
+        return jnp.where(ok, (xg * ly + yl) * nz + cells % nz, lines // 2 * nz)
+
+    first = b == 0
+    enc = code(
+        jnp.stack([jnp.where(first, own_cells, their_cells), jnp.where(first, their_cells, own_cells)]),
+        0, cx,
+    )
+    senc = jnp.stack([code(source_cells[0], -lx * a - cx * h, cx) for h in range(2)])
+    vals = jnp.stack(
+        [jnp.where(first, observed[0], their_obs), jnp.where(first, their_obs, observed[0])]
+    )
+    ones = jnp.ones((2, 1, slots), jnp.float32)
+    vals = jnp.concatenate([vals, ones, jnp.zeros((2, 5, slots), jnp.float32)], axis=1)
     w = wavelet[0]
     gap = jnp.zeros((3, w.shape[1]), jnp.float32)
-    svals = jnp.concatenate([gap, w, gap], axis=0)
+    svals = jnp.concatenate([gap, w, gap], axis=0)[None]
 
     smem = pl.BlockSpec(memory_space=pltpu.SMEM)
     vmem = pl.BlockSpec(memory_space=pltpu.VMEM)
@@ -458,9 +525,17 @@
         scatter_kernel,
         out_shape=(dense, dense, field),
         in_specs=[smem, smem, vmem, vmem],
-        out_specs=(vmem, vmem, vmem),
-        scratch_shapes=[pltpu.VMEM(((lines + 64) * TROWS, nz), f32)],
+        out_specs=(anyw, anyw, anyw),
+        scratch_shapes=[
+            pltpu.VMEM(((lines // 2 + 64) * TROWS, nz), f32),
+            pltpu.VMEM(((lines // 2 + 64) * TROWS, nz), f32),
+            pltpu.VMEM((steps, lx, ly, nz), f32),
+            pltpu.VMEM((steps, lx, ly, nz), f32),
+            pltpu.VMEM((lx, ly, nz), f32),
+            pltpu.SemaphoreType.DMA((3, lx)),
+        ],
         compiler_params=pltpu.CompilerParams(vmem_limit_bytes=48 * 2**20),
+        cost_estimate=pl.CostEstimate(flops=10**9, bytes_accessed=80 * 10**6, transcendentals=0),
         name="scatter",
     )(enc, senc, vals, svals)
 
@@ -470,7 +545,7 @@
     return pl.pallas_call(
         wave_kernel,
         out_shape=jax.ShapeDtypeStruct((cx, band, nz), f32),
-        in_specs=[anyw] * 8,
+        in_specs=[anyw] * 11,
         out_specs=vmem,
         scratch_shapes=[
             pltpu.VMEM((levels, lx + 2 * H, ly + 2 * PAD, nz), f32),
@@ -485,11 +560,10 @@
             pltpu.VMEM((2, cx, band, nz), f32),
             dma((levels, 2 * (ly // CHUNK) + 1)),
             dma((levels, 2 * (ly // CHUNK) + 1)),
-            dma((3,)),
-            dma((3,)),
             dma((2, cx)),
             dma((2, cx)),
-            dma((9,)),
+            dma((13,)),
+            dma((steps,)),
             dma((3,)),
             dma((3,)),
         ],
@@ -497,7 +571,7 @@
             collective_id=0, has_side_effects=True, vmem_limit_bytes=60 * 2**20
         ),
         name="waves",
-    )(velocity, wave_now, wave_prev, adjoint_now, adjoint_prev, s_f, o_f, m_f)
+    )(velocity, wave_now, wave_prev, adjoint_now, adjoint_prev, far, same, cross, s_f, o_f, m_f)
 
 
 def solution(mesh):

time: 175 us -> 156 us (0.89)
  Pallas kernels: 166 us -> 130 us
  waiting for transfers between devices: 0.3 us -> 7.9 us
  starting transfers between devices: 2.08 us -> 9.01 us
  local copies, waits for them, and re-layouts: 4.1 us -> 6.15 us
    pallas_call x1, Pallas kernels: 139 us -> 113 us  [per_device(): pl.pallas_call(wave_kernel, out_shape=jax.ShapeDtypeStruct((cx, band, nz)...]
    pallas_call x1, Pallas kernels: 27.4 us -> 17.9 us  [per_device(): pl.pallas_call(scatter_kernel, out_shape=(dense, dense, field), in_specs=...]
    ppermute x0 -> x3, waiting for transfers between devices: none -> 7.9 us  [the longest x1 7.89 us: per_device(): far = lax.ppermute(far, 'space', swap)]
    ppermute x0 -> x3, starting transfers between devices: none -> 6.99 us  [the longest x1 3.49 us: per_device(): same = lax.ppermute(rows_of(edge, b), 'space', within(beyond))]
    unnamed x5 -> x25, local copies, waits for them, and re-layouts: 3.94 us -> 4.75 us
  transfers between devices with their start and end apart: 2 -> 5, of which waited for: 1 -> 1; matrix products, arithmetic and copies ran while one was open for 1% -> 2% of each run, Pallas kernels for 0% -> 11%
where the time goes in v3:
time: 156 us; the launch traced here: 155 us
  Pallas kernels  130 us (83%)
  starting transfers between devices  9.01 us (6%)
  waiting for transfers between devices  7.9 us (5%)
  local copies, waits for them, and re-layouts  6.15 us (4%)
    pallas_call x1, Pallas kernels, per_device(): pl.pallas_call(wave_kernel, out_shape=jax.ShapeDtypeStruct((cx, band, nz)...  113 us
    pallas_call x1, Pallas kernels, per_device(): pl.pallas_call(scatter_kernel, out_shape=(dense, dense, field), in_specs=...  17.9 us
    ppermute x1, waiting for transfers between devices, per_device(): far = lax.ppermute(far, 'space', swap)  7.89 us
    unnamed x25, local copies, waits for them, and re-layouts  4.75 us
    ppermute x1, starting transfers between devices, per_device(): same = lax.ppermute(rows_of(edge, b), 'space', within(beyond))  3.49 us
    ppermute x1, starting transfers between devices, per_device(): cross = lax.ppermute(rows_of(edge, 1 - b), 'space', within(across))  3.43 us
  transfers between devices with their start and end apart: 5, of which 1 were waited for; matrix products, arithmetic and copies ran while one was open for 2% of the time, Pallas kernels for 11%

profile of v3, /device:TPU:4, one launch (start us, length us, event | category | flops | bytes accessed | tf_op | source)
XLA Modules:
  0.0 155.5 jit_solution(4631916752373019843)
XLA Ops:
  0.0 0.0 copy-start.1
  0.0 0.0 copy-start.2
  0.8 0.7 fusion.2
  1.5 0.0 collective-permute-start.3
  1.5 0.7 copy.19
  2.2 2.0 %collective-permute-start.4 = (f32[10,512]{1,0:T(8,128)S(1)}, f32[10,512]{1,0:T(8,128)S(1)}, u32[]{:S(2)}, u32[]{:S(2)}) collective-permute-start(f32[10,512]{1,0:T(8,128)S(1)} %bitcast.29), channel_id=1, source_target_pairs={{0,4},{4,0},{8,12},{12,8},{16,20},{20,16},{24,28},{28,24},{1,5},{5... | collective-permute-start | bytes 61448 | tf_op jit(solution)/shard_map/ppermute | solution.py:482
  4.2 0.0 copy-start.3
  4.2 1.1 dynamic-slice_bitcast_fusion.1
  5.4 3.4 %collective-permute-start.2 = (f32[4,96,128]{2,1,0:T(8,128)S(1)}, f32[4,96,128]{2,1,0:T(8,128)S(1)}, u32[]{:S(2)}, u32[]{:S(2)}) collective-permute-start(f32[4,96,128]{2,1,0:T(8,128)S(1)} %get-tuple-element.14), channel_id=1, source_target_pairs={{4,8},{8,4},{12,16},{16,12},{20,24},{24,20},{5,9},{9,5},{13,17},{1... | collective-permute-start | bytes 589832 | tf_op jit(solution)/shard_map/ppermute | solution.py:494
  8.8 3.5 %collective-permute-start.1 = (f32[4,96,128]{2,1,0:T(8,128)S(1)}, f32[4,96,128]{2,1,0:T(8,128)S(1)}, u32[]{:S(2)}, u32[]{:S(2)}) collective-permute-start(f32[4,96,128]{2,1,0:T(8,128)S(1)} %get-tuple-element.15), channel_id=1, source_target_pairs={{4,12},{8,0},{12,20},{16,8},{20,28},{24,16},{5,13},{9,1},{13,21},{... | collective-permute-start | bytes 589832 | tf_op jit(solution)/shard_map/ppermute | solution.py:493
  12.3 0.0 copy-done.1
  12.4 0.0 copy-done.2
  12.4 0.0 copy-done.3
  12.5 0.0 copy-start.10
  12.5 0.0 copy-start.9
  12.5 0.0 copy-start.8
  12.5 0.0 copy-start.7
  12.5 0.1 pad_maximum_fusion
  12.6 0.1 collective-permute-start
  12.7 0.4 copy-done.10
  13.1 0.0 copy-done.9
  13.2 0.1 pad.5.clone
  13.3 0.1 pad.6.clone
  13.4 0.0 collective-permute-done.3
  13.4 0.0 copy-done.8
  13.4 0.1 and_select_fusion.1.enc
  13.5 0.0 collective-permute-done.4
  13.5 0.0 copy-done.7
  13.5 0.1 maximum_maximum_fusion.vals
  13.6 17.9 %scatter.1 = (f32[10,16,96,128]{3,2,1,0:T(8,128)}, f32[10,16,96,128]{3,2,1,0:T(8,128)}, f32[16,96,128]{2,1,0:T(8,128)S(1)}) custom-call(s32[2,512]{1,0:T(2,128)S(1)} %and_select_fusion.1.enc, s32[2,128]{1,0:T(2,128)S(1)} %pad_add_fusion.1.senc, f32[2,16,512]{2,1,0:T(8,128)S(1)} %maximum_maximum_fusion.vals, f32[1,16,128]{2,1,0:T(8,128)S(1)} %maximum_bitcast_fusion.svals), custom_call_target="tpu_custom_call" | custom-call | flops 1000000000 | bytes 80000000 | tf_op jit(solution)/shard_map/scatter/pallas_call | solution.py:524
  31.4 0.0 copy-start
  31.5 0.9 copy-done
  32.3 0.0 collective-permute-done.2.cross
  32.4 0.0 copy-start.5
  32.4 0.0 collective-permute-done.1.same
  32.4 0.0 copy-start.6
  32.4 7.9 %collective-permute-done.far = f32[3,8,96,128]{3,2,1,0:T(8,128)S(1)} collective-permute-done((f32[3,8,96,128]{3,2,1,0:T(8,128)S(1)}, f32[3,8,96,128]{3,2,1,0:T(8,128)S(1)}, u32[]{:S(2)}, u32[]{:S(2)}) %collective-permute-start) | collective-permute-done | bytes 1179680 | tf_op jit(solution)/shard_map/ppermute | solution.py:488
  40.3 0.0 copy-start.4
  40.3 0.0 copy-done.5
  40.3 0.0 copy-done.6
  40.3 1.0 copy-done.4
  41.3 112.6 %waves.1 = f32[8,48,128]{2,1,0:T(8,128)} custom-call(f32[8,192,128]{2,1,0:T(8,128)} %vel.1, f32[1,8,192,128]{3,2,1,0:T(8,128)} %now.1, f32[1,8,192,128]{3,2,1,0:T(8,128)} %prev.1, f32[1,8,192,128]{3,2,1,0:T(8,128)} %adj.1, f32[1,8,192,128]{3,2,1,0:T(8,128)} %adjp.1, f32[3,8,96,128]{3,2,1,0:T(8,128)} %copy-done.4, f32[4,96,128]{2,1,0:T(8,128)} %copy-done.6, ...), custom_call_target="tpu_custom_call" | custom-call | tf_op jit(solution)/shard_map/waves/pallas_call | solution.py:545
  153.9 1.6 %copy.23 = f32[8,48,128]{2,1,0:T(8,128)} copy(f32[8,48,128]{2,1,0:T(8,128)} %waves.1) | data formatting | bytes 393216
  (12 shorter events, 0.2 us)
Async XLA Ops:
  0.0 12.3 %copy-start.1 = (f32[1,8,192,128]{3,2,1,0:T(8,128)S(1)}, f32[1,8,192,128]{3,2,1,0:T(8,128)}, u32[]{:S(2)}) copy-start(f32[1,8,192,128]{3,2,1,0:T(8,128)} %now.1) | copy-start | bytes 2359300
  0.0 12.4 %copy-start.2 = (f32[8,192,128]{2,1,0:T(8,128)S(1)}, f32[8,192,128]{2,1,0:T(8,128)}, u32[]{:S(2)}) copy-start(f32[8,192,128]{2,1,0:T(8,128)} %vel.1) | copy-start | bytes 2359300
  1.5 11.9 %collective-permute-start.3 = (s32[512]{0:T(512)S(1)}, s32[512]{0:T(512)S(1)}, u32[]{:S(2)}, u32[]{:S(2)}) collective-permute-start(s32[512]{0:T(512)S(1)} %fusion.2), channel_id=1, source_target_pairs={{0,4},{4,0},{8,12},{12,8},{16,20},{20,16},{24,28},{28,24},{1,5},{5... | collective-permute-start | bytes 6152 | tf_op jit(solution)/shard_map/ppermute | solution.py:481
  2.2 11.3 %collective-permute-start.4 = (f32[10,512]{1,0:T(8,128)S(1)}, f32[10,512]{1,0:T(8,128)S(1)}, u32[]{:S(2)}, u32[]{:S(2)}) collective-permute-start(f32[10,512]{1,0:T(8,128)S(1)} %bitcast.29), channel_id=1, source_target_pairs={{0,4},{4,0},{8,12},{12,8},{16,20},{20,16},{24,28},{28,24},{1,5},{5... | collective-permute-start | bytes 61448 | tf_op jit(solution)/shard_map/ppermute | solution.py:482
  4.2 8.2 %copy-start.3 = (f32[1,8,192,128]{3,2,1,0:T(8,128)S(1)}, f32[1,8,192,128]{3,2,1,0:T(8,128)}, u32[]{:S(2)}) copy-start(f32[1,8,192,128]{3,2,1,0:T(8,128)} %prev.1) | copy-start | bytes 2359300
  5.4 27.0 %collective-permute-start.2 = (f32[4,96,128]{2,1,0:T(8,128)S(1)}, f32[4,96,128]{2,1,0:T(8,128)S(1)}, u32[]{:S(2)}, u32[]{:S(2)}) collective-permute-start(f32[4,96,128]{2,1,0:T(8,128)S(1)} %get-tuple-element.14), channel_id=1, source_target_pairs={{4,8},{8,4},{12,16},{16,12},{20,24},{24,20},{5,9},{9,5},{13,17},{1... | collective-permute-start | bytes 589832 | tf_op jit(solution)/shard_map/ppermute | solution.py:494
  8.8 23.6 %collective-permute-start.1 = (f32[4,96,128]{2,1,0:T(8,128)S(1)}, f32[4,96,128]{2,1,0:T(8,128)S(1)}, u32[]{:S(2)}, u32[]{:S(2)}) collective-permute-start(f32[4,96,128]{2,1,0:T(8,128)S(1)} %get-tuple-element.15), channel_id=1, source_target_pairs={{4,12},{8,0},{12,20},{16,8},{20,28},{24,16},{5,13},{9,1},{13,21},{... | collective-permute-start | bytes 589832 | tf_op jit(solution)/shard_map/ppermute | solution.py:493
  12.5 0.7 copy-start.10
  12.5 0.7 copy-start.9
  12.5 0.9 copy-start.8
  12.5 1.0 copy-start.7
  12.6 27.7 %collective-permute-start = (f32[3,8,96,128]{3,2,1,0:T(8,128)S(1)}, f32[3,8,96,128]{3,2,1,0:T(8,128)S(1)}, u32[]{:S(2)}, u32[]{:S(2)}) collective-permute-start(f32[3,8,96,128]{3,2,1,0:T(8,128)S(1)} %pad_maximum_fusion), channel_id=1, source_target_pairs={{0,4},{4,0},{8,12},{12,8},{16,20},{20,16},{24,28},{28,24},{1,5},{5... | collective-permute-start | bytes 3538952 | tf_op jit(solution)/shard_map/ppermute | solution.py:488
  31.4 0.9 copy-start
  32.4 7.9 %copy-start.5 = (f32[4,96,128]{2,1,0:T(8,128)}, f32[4,96,128]{2,1,0:T(8,128)S(1)}, u32[]{:S(2)}) copy-start(f32[4,96,128]{2,1,0:T(8,128)S(1)} %collective-permute-done.2.cross) | copy-start | bytes 589828
  32.4 7.9 %copy-start.6 = (f32[4,96,128]{2,1,0:T(8,128)}, f32[4,96,128]{2,1,0:T(8,128)S(1)}, u32[]{:S(2)}) copy-start(f32[4,96,128]{2,1,0:T(8,128)S(1)} %collective-permute-done.1.same) | copy-start | bytes 589828
  40.3 1.0 copy-start.4

commit v4 on v3

--- a/solution.py
+++ b/solution.py
@@ -13,7 +13,8 @@
 PAD = 8
 H = 4
 TROWS = 21
-CHUNK = 32
+CHUNK = 24
+PIECE = 48
 
 
 def scatter_kernel(
@@ -90,7 +91,7 @@
 
 def wave_kernel(
     vel, now, prev, adj, adjp, far, same, cross, s_hbm, o_hbm, m_hbm, out,
-    u, c2, velb, s_v, o_v, m_v, img, pair, red, got,
+    u, c2, s_v, o_v, m_v, img, pair, red, got,
     halo_send, halo_recv, adj_send, adj_recv, loc, s_sem, red_send, red_recv,
 ):
     cx, ny, nz = vel.shape
@@ -182,9 +183,6 @@
 
     extra = [
         pltpu.make_async_copy(m_hbm, m_v, loc.at[5]),
-        pltpu.make_async_copy(
-            vel.at[:, pl.ds(pl.multiple_of(velb.shape[1] * s, 8), velb.shape[1]), :], velb, loc.at[6]
-        ),
         pltpu.make_async_copy(o_hbm, o_v, loc.at[7]),
     ]
 
@@ -225,10 +223,10 @@
     pl.semaphore_wait(barrier, 4 + has_low.astype(jnp.int32) + has_high.astype(jnp.int32))
 
 
-    pieces = ly // CHUNK
+    pieces = ly // PIECE
 
     def send_up(l, p):
-        rows = slice(PAD + CHUNK * p, PAD + CHUNK * (p + 1))
+        rows = slice(PAD + PIECE * p, PAD + PIECE * (p + 1))
         return pltpu.make_async_remote_copy(
             src_ref=u.at[l, lx : lx + H, rows, :],
             dst_ref=u.at[l, 0:H, rows, :],
@@ -237,7 +235,7 @@
         )
 
     def send_down(l, p):
-        rows = slice(PAD + CHUNK * p, PAD + CHUNK * (p + 1))
+        rows = slice(PAD + PIECE * p, PAD + PIECE * (p + 1))
         return pltpu.make_async_remote_copy(
             src_ref=u.at[l, H : 2 * H, rows, :],
             dst_ref=u.at[l, lx + H : lx + 2 * H, rows, :],
@@ -290,21 +288,28 @@
     def laplace(l, xi, r0):
         rows = lambda d: slice(PAD + r0 + d, PAD + r0 + d + CHUNK)
         centre = u[l, H + xi, rows(0), :]
+        up = lambda v, k: jnp.where(lane >= k, pltpu.roll(v, k, 1), 0.0)
+        down = lambda v, k: jnp.where(lane < nz - k, pltpu.roll(v, nz - k, 1), 0.0)
+        up1, up2, down1, down2 = up(centre, 1), up(centre, 2), down(centre, 1), down(centre, 2)
+        along = {1: up1 + down1, 2: up2 + down2}
         result = 3.0 * TAPS[0] * centre
         for k in range(1, H + 1):
             beside = u[l, H + xi + k, rows(0), :] + u[l, H + xi - k, rows(0), :]
-            beside = beside + u[l, H + xi, rows(k), :] + u[l, H + xi, rows(-k), :]
-            beside = beside + jnp.where(lane < nz - k, pltpu.roll(centre, nz - k, 1), 0.0)
-            beside = beside + jnp.where(lane >= k, pltpu.roll(centre, k, 1), 0.0)
+            beside = beside + (u[l, H + xi, rows(k), :] + u[l, H + xi, rows(-k), :])
+            if k in along:
+                beside = beside + along[k]
             result = result + TAPS[k] * beside
+        result = result + up(TAPS[3] * up1 + TAPS[4] * up2, 2)
+        result = result + down(TAPS[3] * down1 + TAPS[4] * down2, 2)
         return centre, result
 
     def sweep(first, last, p, body):
         def layer(xi, _):
-            body(xi, CHUNK * p)
+            for r0 in range(PIECE * p, PIECE * (p + 1), CHUNK):
+                body(xi, r0)
             return 0
 
-        lax.fori_loop(first, last, layer, 0, unroll=2)
+        lax.fori_loop(first, last, layer, 0)
 
     def step(cur, arrives, more, order, cell):
         for n, p in enumerate(order):
@@ -407,7 +412,7 @@
     def _():
         both(tuple(range(pieces)))
 
-    band = velb.shape[1]
+    band = out.shape[1]
     keep = pl.multiple_of(band * core, 8)
     give = pl.multiple_of(band * (1 - core), 8)
     swap = pltpu.make_async_remote_copy(
@@ -458,8 +463,7 @@
             deliver(k).wait_send()
 
     for xi in range(cx):
-        v = velb[xi]
-        out[xi] = (-2.0 / (v * v * v)) * (got[0, xi] + got[1, xi])
+        out[xi] = got[0, xi] + got[1, xi]
 
 
 def per_device(
@@ -542,7 +546,7 @@
     levels = 2 * steps + 4
     band = ny // 4
     dma = pltpu.SemaphoreType.DMA
-    return pl.pallas_call(
+    image = pl.pallas_call(
         wave_kernel,
         out_shape=jax.ShapeDtypeStruct((cx, band, nz), f32),
         in_specs=[anyw] * 11,
@@ -550,7 +554,6 @@
         scratch_shapes=[
             pltpu.VMEM((levels, lx + 2 * H, ly + 2 * PAD, nz), f32),
             pltpu.VMEM((lx, ly, nz), f32),
-            pltpu.VMEM((cx, band, nz), f32),
             pltpu.VMEM((steps, lx, ly, nz), f32),
             pltpu.VMEM((steps, lx, ly, nz), f32),
             pltpu.VMEM((lx, ly, nz), f32),
@@ -558,8 +561,8 @@
             pltpu.VMEM((lx, band, nz), f32),
             pltpu.VMEM((lx, band, nz), f32),
             pltpu.VMEM((2, cx, band, nz), f32),
-            dma((levels, 2 * (ly // CHUNK) + 1)),
-            dma((levels, 2 * (ly // CHUNK) + 1)),
+            dma((levels, 2 * (ly // PIECE) + 1)),
+            dma((levels, 2 * (ly // PIECE) + 1)),
             dma((2, cx)),
             dma((2, cx)),
             dma((13,)),
@@ -572,6 +575,8 @@
         ),
         name="waves",
     )(velocity, wave_now, wave_prev, adjoint_now, adjoint_prev, far, same, cross, s_f, o_f, m_f)
+    own = lax.dynamic_slice_in_dim(velocity, lax.axis_index("shot") * band, band, 1)
+    return -2.0 / (own * own * own) * image
 
 
 def solution(mesh):

time: 156 us -> 186 us (1.19)
  Pallas kernels: 130 us -> 160 us
    pallas_call x1, Pallas kernels: 113 us -> 142 us  [per_device(): pl.pallas_call(wave_kernel, out_shape=jax.ShapeDtypeStruct((cx, band, nz)...]
    unnamed x25 -> x24, local copies, waits for them, and re-layouts: 4.75 us -> 3.14 us
  transfers between devices with their start and end apart: 5 -> 5, of which waited for: 1 -> 1; matrix products, arithmetic and copies ran while one was open for 2% -> 1% of each run, Pallas kernels for 11% -> 10%
where the time goes in v4:
time: 186 us; the launch traced here: 185 us
  Pallas kernels  160 us (86%)
  starting transfers between devices  9.01 us (5%)
  waiting for transfers between devices  7.91 us (4%)
  local copies, waits for them, and re-layouts  4.54 us (2%)
  other arithmetic  2.72 us (1%)
    pallas_call x1, Pallas kernels, per_device(): pl.pallas_call(wave_kernel, out_shape=jax.ShapeDtypeStruct((cx, band, nz)...  142 us
    pallas_call x1, Pallas kernels, per_device(): pl.pallas_call(scatter_kernel, out_shape=(dense, dense, field), in_specs=...  17.9 us
    ppermute x1, waiting for transfers between devices, per_device(): far = lax.ppermute(far, 'space', swap)  7.9 us
  transfers between devices with their start and end apart: 5, of which 1 were waited for; matrix products, arithmetic and copies ran while one was open for 1% of the time, Pallas kernels for 10%

profile of v4, /device:TPU:4, one launch (start us, length us, event | category | flops | bytes accessed | tf_op | source)
XLA Modules:
  0.0 185.3 jit_solution(2231832318467366299)
XLA Ops:
  0.0 0.0 copy-start.1
  0.0 0.0 copy-start.3
  0.8 0.7 fusion.4
  1.5 0.0 collective-permute-start.3
  1.5 0.7 copy.19
  2.2 2.0 %collective-permute-start.4 = (f32[10,512]{1,0:T(8,128)S(1)}, f32[10,512]{1,0:T(8,128)S(1)}, u32[]{:S(2)}, u32[]{:S(2)}) collective-permute-start(f32[10,512]{1,0:T(8,128)S(1)} %bitcast.29), channel_id=1, source_target_pairs={{0,4},{4,0},{8,12},{12,8},{16,20},{20,16},{24,28},{28,24},{1,5},{5... | collective-permute-start | bytes 61448 | tf_op jit(solution)/shard_map/ppermute | solution.py:486
  4.2 0.0 copy-start.2
  4.2 1.1 dynamic-slice_bitcast_fusion.1
  5.4 3.4 %collective-permute-start.2 = (f32[4,96,128]{2,1,0:T(8,128)S(1)}, f32[4,96,128]{2,1,0:T(8,128)S(1)}, u32[]{:S(2)}, u32[]{:S(2)}) collective-permute-start(f32[4,96,128]{2,1,0:T(8,128)S(1)} %get-tuple-element.14), channel_id=1, source_target_pairs={{4,8},{8,4},{12,16},{16,12},{20,24},{24,20},{5,9},{9,5},{13,17},{1... | collective-permute-start | bytes 589832 | tf_op jit(solution)/shard_map/ppermute | solution.py:498
  8.8 3.5 %collective-permute-start.1 = (f32[4,96,128]{2,1,0:T(8,128)S(1)}, f32[4,96,128]{2,1,0:T(8,128)S(1)}, u32[]{:S(2)}, u32[]{:S(2)}) collective-permute-start(f32[4,96,128]{2,1,0:T(8,128)S(1)} %get-tuple-element.15), channel_id=1, source_target_pairs={{4,12},{8,0},{12,20},{16,8},{20,28},{24,16},{5,13},{9,1},{13,21},{... | collective-permute-start | bytes 589832 | tf_op jit(solution)/shard_map/ppermute | solution.py:497
  12.3 0.0 copy-done.1
  12.4 0.0 copy-done.3
  12.4 0.0 copy-done.2
  12.5 0.0 copy-start.10
  12.5 0.0 copy-start.9
  12.5 0.0 copy-start.8
  12.5 0.0 copy-start.7
  12.5 0.1 pad_maximum_fusion
  12.6 0.1 collective-permute-start
  12.7 0.4 copy-done.10
  13.1 0.0 copy-done.9
  13.2 0.1 pad.5.clone
  13.3 0.1 pad.6.clone
  13.4 0.0 collective-permute-done.3
  13.4 0.0 copy-done.8
  13.4 0.1 and_select_fusion.1.enc
  13.5 0.0 collective-permute-done.4
  13.5 0.0 copy-done.7
  13.5 0.1 maximum_maximum_fusion.vals
  13.6 17.9 %scatter.1 = (f32[10,16,96,128]{3,2,1,0:T(8,128)}, f32[10,16,96,128]{3,2,1,0:T(8,128)}, f32[16,96,128]{2,1,0:T(8,128)S(1)}) custom-call(s32[2,512]{1,0:T(2,128)S(1)} %and_select_fusion.1.enc, s32[2,128]{1,0:T(2,128)S(1)} %pad_add_fusion.1.senc, f32[2,16,512]{2,1,0:T(8,128)S(1)} %maximum_maximum_fusion.vals, f32[1,16,128]{2,1,0:T(8,128)S(1)} %maximum_bitcast_fusion.svals), custom_call_target="tpu_custom_call" | custom-call | flops 1000000000 | bytes 80000000 | tf_op jit(solution)/shard_map/scatter/pallas_call | solution.py:528
  31.4 0.0 copy-start
  31.5 0.9 copy-done
  32.3 0.0 collective-permute-done.2.cross
  32.3 0.0 copy-start.5
  32.3 0.0 collective-permute-done.1.same
  32.4 0.0 copy-start.6
  32.4 7.9 %collective-permute-done.far = f32[3,8,96,128]{3,2,1,0:T(8,128)S(1)} collective-permute-done((f32[3,8,96,128]{3,2,1,0:T(8,128)S(1)}, f32[3,8,96,128]{3,2,1,0:T(8,128)S(1)}, u32[]{:S(2)}, u32[]{:S(2)}) %collective-permute-start) | collective-permute-done | bytes 1179680 | tf_op jit(solution)/shard_map/ppermute | solution.py:492
  40.3 0.0 copy-start.4
  40.3 0.0 copy-done.5
  40.3 0.0 copy-done.6
  40.3 1.0 copy-done.4
  41.3 142.2 %waves.1 = f32[8,48,128]{2,1,0:T(8,128)} custom-call(f32[8,192,128]{2,1,0:T(8,128)} %vel.1, f32[1,8,192,128]{3,2,1,0:T(8,128)} %now.1, f32[1,8,192,128]{3,2,1,0:T(8,128)} %prev.1, f32[1,8,192,128]{3,2,1,0:T(8,128)} %adj.1, f32[1,8,192,128]{3,2,1,0:T(8,128)} %adjp.1, f32[3,8,96,128]{3,2,1,0:T(8,128)} %copy-done.4, f32[4,96,128]{2,1,0:T(8,128)} %copy-done.6, ...), custom_call_target="tpu_custom_call" | custom-call | tf_op jit(solution)/shard_map/waves/pallas_call | solution.py:549
  183.5 1.7 fusion.1
  (12 shorter events, 0.2 us)
Async XLA Ops:
  0.0 12.3 %copy-start.1 = (f32[1,8,192,128]{3,2,1,0:T(8,128)S(1)}, f32[1,8,192,128]{3,2,1,0:T(8,128)}, u32[]{:S(2)}) copy-start(f32[1,8,192,128]{3,2,1,0:T(8,128)} %now.1) | copy-start | bytes 2359300
  0.0 12.4 %copy-start.3 = (f32[1,8,192,128]{3,2,1,0:T(8,128)S(1)}, f32[1,8,192,128]{3,2,1,0:T(8,128)}, u32[]{:S(2)}) copy-start(f32[1,8,192,128]{3,2,1,0:T(8,128)} %prev.1) | copy-start | bytes 2359300
  1.5 11.9 %collective-permute-start.3 = (s32[512]{0:T(512)S(1)}, s32[512]{0:T(512)S(1)}, u32[]{:S(2)}, u32[]{:S(2)}) collective-permute-start(s32[512]{0:T(512)S(1)} %fusion.4), channel_id=1, source_target_pairs={{0,4},{4,0},{8,12},{12,8},{16,20},{20,16},{24,28},{28,24},{1,5},{5... | collective-permute-start | bytes 6152 | tf_op jit(solution)/shard_map/ppermute | solution.py:485
  2.2 11.3 %collective-permute-start.4 = (f32[10,512]{1,0:T(8,128)S(1)}, f32[10,512]{1,0:T(8,128)S(1)}, u32[]{:S(2)}, u32[]{:S(2)}) collective-permute-start(f32[10,512]{1,0:T(8,128)S(1)} %bitcast.29), channel_id=1, source_target_pairs={{0,4},{4,0},{8,12},{12,8},{16,20},{20,16},{24,28},{28,24},{1,5},{5... | collective-permute-start | bytes 61448 | tf_op jit(solution)/shard_map/ppermute | solution.py:486
  4.2 8.2 %copy-start.2 = (f32[8,192,128]{2,1,0:T(8,128)S(1)}, f32[8,192,128]{2,1,0:T(8,128)}, u32[]{:S(2)}) copy-start(f32[8,192,128]{2,1,0:T(8,128)} %vel.1) | copy-start | bytes 2359300
  5.4 27.0 %collective-permute-start.2 = (f32[4,96,128]{2,1,0:T(8,128)S(1)}, f32[4,96,128]{2,1,0:T(8,128)S(1)}, u32[]{:S(2)}, u32[]{:S(2)}) collective-permute-start(f32[4,96,128]{2,1,0:T(8,128)S(1)} %get-tuple-element.14), channel_id=1, source_target_pairs={{4,8},{8,4},{12,16},{16,12},{20,24},{24,20},{5,9},{9,5},{13,17},{1... | collective-permute-start | bytes 589832 | tf_op jit(solution)/shard_map/ppermute | solution.py:498
  8.8 23.6 %collective-permute-start.1 = (f32[4,96,128]{2,1,0:T(8,128)S(1)}, f32[4,96,128]{2,1,0:T(8,128)S(1)}, u32[]{:S(2)}, u32[]{:S(2)}) collective-permute-start(f32[4,96,128]{2,1,0:T(8,128)S(1)} %get-tuple-element.15), channel_id=1, source_target_pairs={{4,12},{8,0},{12,20},{16,8},{20,28},{24,16},{5,13},{9,1},{13,21},{... | collective-permute-start | bytes 589832 | tf_op jit(solution)/shard_map/ppermute | solution.py:497
  12.5 0.7 copy-start.10
  12.5 0.7 copy-start.9
  12.5 0.9 copy-start.8
  12.5 1.0 copy-start.7
  12.6 27.7 %collective-permute-start = (f32[3,8,96,128]{3,2,1,0:T(8,128)S(1)}, f32[3,8,96,128]{3,2,1,0:T(8,128)S(1)}, u32[]{:S(2)}, u32[]{:S(2)}) collective-permute-start(f32[3,8,96,128]{3,2,1,0:T(8,128)S(1)} %pad_maximum_fusion), channel_id=1, source_target_pairs={{0,4},{4,0},{8,12},{12,8},{16,20},{20,16},{24,28},{28,24},{1,5},{5... | collective-permute-start | bytes 3538952 | tf_op jit(solution)/shard_map/ppermute | solution.py:492
  31.4 0.9 copy-start
  32.3 7.9 %copy-start.5 = (f32[4,96,128]{2,1,0:T(8,128)}, f32[4,96,128]{2,1,0:T(8,128)S(1)}, u32[]{:S(2)}) copy-start(f32[4,96,128]{2,1,0:T(8,128)S(1)} %collective-permute-done.2.cross) | copy-start | bytes 589828
  32.4 7.9 %copy-start.6 = (f32[4,96,128]{2,1,0:T(8,128)}, f32[4,96,128]{2,1,0:T(8,128)S(1)}, u32[]{:S(2)}) copy-start(f32[4,96,128]{2,1,0:T(8,128)S(1)} %collective-permute-done.1.same) | copy-start | bytes 589828
  40.3 1.0 copy-start.4

commit v5 on v4

--- a/solution.py
+++ b/solution.py
@@ -13,8 +13,9 @@
 PAD = 8
 H = 4
 TROWS = 21
-CHUNK = 24
-PIECE = 48
+CHUNK = 32
+PIECE = 32
+GROUP = 4
 
 
 def scatter_kernel(
@@ -288,28 +289,29 @@
     def laplace(l, xi, r0):
         rows = lambda d: slice(PAD + r0 + d, PAD + r0 + d + CHUNK)
         centre = u[l, H + xi, rows(0), :]
-        up = lambda v, k: jnp.where(lane >= k, pltpu.roll(v, k, 1), 0.0)
-        down = lambda v, k: jnp.where(lane < nz - k, pltpu.roll(v, nz - k, 1), 0.0)
-        up1, up2, down1, down2 = up(centre, 1), up(centre, 2), down(centre, 1), down(centre, 2)
-        along = {1: up1 + down1, 2: up2 + down2}
         result = 3.0 * TAPS[0] * centre
         for k in range(1, H + 1):
             beside = u[l, H + xi + k, rows(0), :] + u[l, H + xi - k, rows(0), :]
             beside = beside + (u[l, H + xi, rows(k), :] + u[l, H + xi, rows(-k), :])
-            if k in along:
-                beside = beside + along[k]
-            result = result + TAPS[k] * beside
-        result = result + up(TAPS[3] * up1 + TAPS[4] * up2, 2)
-        result = result + down(TAPS[3] * down1 + TAPS[4] * down2, 2)
+            above = jnp.where(lane < nz - k, pltpu.roll(centre, nz - k, 1), 0.0)
+            below = jnp.where(lane >= k, pltpu.roll(centre, k, 1), 0.0)
+            result = result + TAPS[k] * (beside + (above + below))
         return centre, result
 
     def sweep(first, last, p, body):
-        def layer(xi, _):
-            for r0 in range(PIECE * p, PIECE * (p + 1), CHUNK):
-                body(xi, r0)
+        def group(g, _):
+            writes = []
+            for j in range(GROUP):
+                writes += body(first + g * GROUP + j, PIECE * p)
+            for ref, at, value in writes:
+                ref[at] = value
             return 0
 
-        lax.fori_loop(first, last, layer, 0)
+        count = (last - first) // GROUP
+        if count == 1:
+            group(0, 0)
+        else:
+            lax.fori_loop(0, count, group, 0)
 
     def step(cur, arrives, more, order, cell):
         for n, p in enumerate(order):
@@ -338,8 +340,8 @@
 
     def square(xi, r0):
         value = COURANT * c2[xi, r0 : r0 + CHUNK, :]
-        c2[xi, r0 : r0 + CHUNK, :] = value * value
-        img[xi, r0 : r0 + CHUNK, :] = jnp.zeros((CHUNK, nz), jnp.float32)
+        at = (xi, slice(r0, r0 + CHUNK))
+        return [(c2, at, value * value), (img, at, jnp.zeros((CHUNK, nz), jnp.float32))]
 
     def forward(order, t, _):
         cur = t + 1
@@ -349,7 +351,7 @@
             inner = slice(r0, r0 + CHUNK)
             centre, lap = laplace(cur, xi, r0)
             fresh = 2.0 * centre - u[t, H + xi, rows, :] + c2[xi, inner, :] * lap
-            u[t + 2, H + xi, rows, :] = fresh + s_v[t, xi, inner, :]
+            return [(u, (t + 2, H + xi, rows), fresh + s_v[t, xi, inner, :])]
 
         @pl.when(t < cx)
         def _():
@@ -385,8 +387,8 @@
             later = u[t + 2, H + xi, rows, :]
             fresh = fresh + m_v[xi, inner, :] * (later - o_v[t, xi, inner, :])
             accel = later - 2.0 * u[t + 1, H + xi, rows, :] + u[t, H + xi, rows, :]
-            img[xi, inner, :] = img[xi, inner, :] + fresh * accel
-            u[cur + 1, H + xi, rows, :] = fresh
+            total = img[xi, inner, :] + fresh * accel
+            return [(img, (xi, inner), total), (u, (cur + 1, H + xi, rows), fresh)]
 
         step(cur, True, k < steps - 1, order, cell)
         return 0

time: 186 us -> 150 us (0.81)
  Pallas kernels: 160 us -> 125 us
    pallas_call x1, Pallas kernels: 142 us -> 107 us  [per_device(): pl.pallas_call(wave_kernel, out_shape=jax.ShapeDtypeStruct((cx, band, nz)...]
  transfers between devices with their start and end apart: 5 -> 5, of which waited for: 1 -> 1; matrix products, arithmetic and copies ran while one was open for 1% -> 2% of each run, Pallas kernels for 10% -> 12%
where the time goes in v5:
time: 150 us
  Pallas kernels  125 us (83%)
  starting transfers between devices  9.01 us (6%)
  waiting for transfers between devices  7.83 us (5%)
  local copies, waits for them, and re-layouts  4.54 us (3%)
  other arithmetic  2.72 us (2%)
    pallas_call x1, Pallas kernels, per_device(): pl.pallas_call(wave_kernel, out_shape=jax.ShapeDtypeStruct((cx, band, nz)...  107 us
    pallas_call x1, Pallas kernels, per_device(): pl.pallas_call(scatter_kernel, out_shape=(dense, dense, field), in_specs=...  17.9 us
    ppermute x1, waiting for transfers between devices, per_device(): far = lax.ppermute(far, 'space', swap)  7.82 us
    ppermute x1, starting transfers between devices, per_device(): same = lax.ppermute(rows_of(edge, b), 'space', within(beyond))  3.49 us
    ppermute x1, starting transfers between devices, per_device(): cross = lax.ppermute(rows_of(edge, 1 - b), 'space', within(across))  3.43 us
    unnamed x24, local copies, waits for them, and re-layouts  3.14 us
  transfers between devices with their start and end apart: 5, of which 1 were waited for; matrix products, arithmetic and copies ran while one was open for 2% of the time, Pallas kernels for 12%

profile of v5, /device:TPU:4, one launch (start us, length us, event | category | flops | bytes accessed | tf_op | source)
XLA Modules:
  0.0 150.1 jit_solution(14376028441550083171)
XLA Ops:
  0.0 0.0 copy-start.1
  0.0 0.0 copy-start.3
  0.8 0.7 fusion.4
  1.5 0.0 collective-permute-start.3
  1.5 0.7 copy.19
  2.2 2.0 %collective-permute-start.4 = (f32[10,512]{1,0:T(8,128)S(1)}, f32[10,512]{1,0:T(8,128)S(1)}, u32[]{:S(2)}, u32[]{:S(2)}) collective-permute-start(f32[10,512]{1,0:T(8,128)S(1)} %bitcast.29), channel_id=1, source_target_pairs={{0,4},{4,0},{8,12},{12,8},{16,20},{20,16},{24,28},{28,24},{1,5},{5... | collective-permute-start | bytes 61448 | tf_op jit(solution)/shard_map/ppermute | solution.py:488
  4.2 0.0 copy-start.2
  4.2 1.1 dynamic-slice_bitcast_fusion.1
  5.4 3.4 %collective-permute-start.2 = (f32[4,96,128]{2,1,0:T(8,128)S(1)}, f32[4,96,128]{2,1,0:T(8,128)S(1)}, u32[]{:S(2)}, u32[]{:S(2)}) collective-permute-start(f32[4,96,128]{2,1,0:T(8,128)S(1)} %get-tuple-element.14), channel_id=1, source_target_pairs={{4,8},{8,4},{12,16},{16,12},{20,24},{24,20},{5,9},{9,5},{13,17},{1... | collective-permute-start | bytes 589832 | tf_op jit(solution)/shard_map/ppermute | solution.py:500
  8.8 3.5 %collective-permute-start.1 = (f32[4,96,128]{2,1,0:T(8,128)S(1)}, f32[4,96,128]{2,1,0:T(8,128)S(1)}, u32[]{:S(2)}, u32[]{:S(2)}) collective-permute-start(f32[4,96,128]{2,1,0:T(8,128)S(1)} %get-tuple-element.15), channel_id=1, source_target_pairs={{4,12},{8,0},{12,20},{16,8},{20,28},{24,16},{5,13},{9,1},{13,21},{... | collective-permute-start | bytes 589832 | tf_op jit(solution)/shard_map/ppermute | solution.py:499
  12.3 0.0 copy-done.1
  12.4 0.0 copy-done.3
  12.4 0.0 copy-done.2
  12.5 0.0 copy-start.10
  12.5 0.0 copy-start.9
  12.5 0.0 copy-start.8
  12.5 0.0 copy-start.7
  12.5 0.1 pad_maximum_fusion
  12.6 0.1 collective-permute-start
  12.7 0.4 copy-done.10
  13.1 0.0 copy-done.9
  13.2 0.1 pad.5.clone
  13.3 0.1 pad.6.clone
  13.4 0.0 collective-permute-done.3
  13.4 0.0 copy-done.8
  13.4 0.1 and_select_fusion.1.enc
  13.5 0.0 collective-permute-done.4
  13.5 0.0 copy-done.7
  13.5 0.1 maximum_maximum_fusion.vals
  13.6 17.9 %scatter.1 = (f32[10,16,96,128]{3,2,1,0:T(8,128)}, f32[10,16,96,128]{3,2,1,0:T(8,128)}, f32[16,96,128]{2,1,0:T(8,128)S(1)}) custom-call(s32[2,512]{1,0:T(2,128)S(1)} %and_select_fusion.1.enc, s32[2,128]{1,0:T(2,128)S(1)} %pad_add_fusion.1.senc, f32[2,16,512]{2,1,0:T(8,128)S(1)} %maximum_maximum_fusion.vals, f32[1,16,128]{2,1,0:T(8,128)S(1)} %maximum_bitcast_fusion.svals), custom_call_target="tpu_custom_call" | custom-call | flops 1000000000 | bytes 80000000 | tf_op jit(solution)/shard_map/scatter/pallas_call | solution.py:530
  31.5 0.0 copy-start
  31.5 0.9 copy-done
  32.4 0.0 collective-permute-done.2.cross
  32.4 0.0 copy-start.5
  32.4 0.0 collective-permute-done.1.same
  32.4 0.0 copy-start.6
  32.4 7.8 %collective-permute-done.far = f32[3,8,96,128]{3,2,1,0:T(8,128)S(1)} collective-permute-done((f32[3,8,96,128]{3,2,1,0:T(8,128)S(1)}, f32[3,8,96,128]{3,2,1,0:T(8,128)S(1)}, u32[]{:S(2)}, u32[]{:S(2)}) %collective-permute-start) | collective-permute-done | bytes 1179680 | tf_op jit(solution)/shard_map/ppermute | solution.py:494
  40.3 0.0 copy-start.4
  40.3 0.0 copy-done.5
  40.3 0.0 copy-done.6
  40.3 1.0 copy-done.4
  41.3 107.0 %waves.1 = f32[8,48,128]{2,1,0:T(8,128)} custom-call(f32[8,192,128]{2,1,0:T(8,128)} %vel.1, f32[1,8,192,128]{3,2,1,0:T(8,128)} %now.1, f32[1,8,192,128]{3,2,1,0:T(8,128)} %prev.1, f32[1,8,192,128]{3,2,1,0:T(8,128)} %adj.1, f32[1,8,192,128]{3,2,1,0:T(8,128)} %adjp.1, f32[3,8,96,128]{3,2,1,0:T(8,128)} %copy-done.4, f32[4,96,128]{2,1,0:T(8,128)} %copy-done.6, ...), custom_call_target="tpu_custom_call" | custom-call | tf_op jit(solution)/shard_map/waves/pallas_call | solution.py:551
  148.3 1.7 %fusion.1 = f32[8,48,128]{2,1,0:T(8,128)} fusion(f32[8,48,128]{2,1,0:T(8,128)} %waves.1, f32[8,192,128]{2,1,0:T(8,128)} %vel.1, s32[]{:T(128)S(6)} %select_n.123), kind=kLoop, calls=%fused_computation.4 | loop fusion | flops 196608 | bytes 589828 | tf_op jit(solution)/shard_map/mul | solution.py:581
  (12 shorter events, 0.2 us)
Async XLA Ops:
  0.0 12.3 %copy-start.1 = (f32[1,8,192,128]{3,2,1,0:T(8,128)S(1)}, f32[1,8,192,128]{3,2,1,0:T(8,128)}, u32[]{:S(2)}) copy-start(f32[1,8,192,128]{3,2,1,0:T(8,128)} %now.1) | copy-start | bytes 2359300
  0.0 12.4 %copy-start.3 = (f32[1,8,192,128]{3,2,1,0:T(8,128)S(1)}, f32[1,8,192,128]{3,2,1,0:T(8,128)}, u32[]{:S(2)}) copy-start(f32[1,8,192,128]{3,2,1,0:T(8,128)} %prev.1) | copy-start | bytes 2359300
  1.5 11.9 %collective-permute-start.3 = (s32[512]{0:T(512)S(1)}, s32[512]{0:T(512)S(1)}, u32[]{:S(2)}, u32[]{:S(2)}) collective-permute-start(s32[512]{0:T(512)S(1)} %fusion.4), channel_id=1, source_target_pairs={{0,4},{4,0},{8,12},{12,8},{16,20},{20,16},{24,28},{28,24},{1,5},{5... | collective-permute-start | bytes 6152 | tf_op jit(solution)/shard_map/ppermute | solution.py:487
  2.2 11.3 %collective-permute-start.4 = (f32[10,512]{1,0:T(8,128)S(1)}, f32[10,512]{1,0:T(8,128)S(1)}, u32[]{:S(2)}, u32[]{:S(2)}) collective-permute-start(f32[10,512]{1,0:T(8,128)S(1)} %bitcast.29), channel_id=1, source_target_pairs={{0,4},{4,0},{8,12},{12,8},{16,20},{20,16},{24,28},{28,24},{1,5},{5... | collective-permute-start | bytes 61448 | tf_op jit(solution)/shard_map/ppermute | solution.py:488
  4.2 8.2 %copy-start.2 = (f32[8,192,128]{2,1,0:T(8,128)S(1)}, f32[8,192,128]{2,1,0:T(8,128)}, u32[]{:S(2)}) copy-start(f32[8,192,128]{2,1,0:T(8,128)} %vel.1) | copy-start | bytes 2359300
  5.4 27.1 %collective-permute-start.2 = (f32[4,96,128]{2,1,0:T(8,128)S(1)}, f32[4,96,128]{2,1,0:T(8,128)S(1)}, u32[]{:S(2)}, u32[]{:S(2)}) collective-permute-start(f32[4,96,128]{2,1,0:T(8,128)S(1)} %get-tuple-element.14), channel_id=1, source_target_pairs={{4,8},{8,4},{12,16},{16,12},{20,24},{24,20},{5,9},{9,5},{13,17},{1... | collective-permute-start | bytes 589832 | tf_op jit(solution)/shard_map/ppermute | solution.py:500
  8.8 23.6 %collective-permute-start.1 = (f32[4,96,128]{2,1,0:T(8,128)S(1)}, f32[4,96,128]{2,1,0:T(8,128)S(1)}, u32[]{:S(2)}, u32[]{:S(2)}) collective-permute-start(f32[4,96,128]{2,1,0:T(8,128)S(1)} %get-tuple-element.15), channel_id=1, source_target_pairs={{4,12},{8,0},{12,20},{16,8},{20,28},{24,16},{5,13},{9,1},{13,21},{... | collective-permute-start | bytes 589832 | tf_op jit(solution)/shard_map/ppermute | solution.py:499
  12.5 0.7 copy-start.10
  12.5 0.7 copy-start.9
  12.5 0.9 copy-start.8
  12.5 1.0 copy-start.7
  12.6 27.7 %collective-permute-start = (f32[3,8,96,128]{3,2,1,0:T(8,128)S(1)}, f32[3,8,96,128]{3,2,1,0:T(8,128)S(1)}, u32[]{:S(2)}, u32[]{:S(2)}) collective-permute-start(f32[3,8,96,128]{3,2,1,0:T(8,128)S(1)} %pad_maximum_fusion), channel_id=1, source_target_pairs={{0,4},{4,0},{8,12},{12,8},{16,20},{20,16},{24,28},{28,24},{1,5},{5... | collective-permute-start | bytes 3538952 | tf_op jit(solution)/shard_map/ppermute | solution.py:494
  31.5 0.9 copy-start
  32.4 7.8 %copy-start.5 = (f32[4,96,128]{2,1,0:T(8,128)}, f32[4,96,128]{2,1,0:T(8,128)S(1)}, u32[]{:S(2)}) copy-start(f32[4,96,128]{2,1,0:T(8,128)S(1)} %collective-permute-done.2.cross) | copy-start | bytes 589828
  32.4 7.8 %copy-start.6 = (f32[4,96,128]{2,1,0:T(8,128)}, f32[4,96,128]{2,1,0:T(8,128)S(1)}, u32[]{:S(2)}) copy-start(f32[4,96,128]{2,1,0:T(8,128)S(1)} %collective-permute-done.1.same) | copy-start | bytes 589828
  40.3 1.0 copy-start.4

commit v6 on v5

--- a/solution.py
+++ b/solution.py
@@ -160,8 +160,19 @@
     def local_copy(k):
         return pltpu.make_async_copy(view(k, mine), landing(k, b), loc.at[k])
 
+    part = pl.ds(cx * (1 - b) + (cx // 2) * core, cx // 2)
+
     def far_copy(k):
-        return pltpu.make_async_copy(far.at[k], landing(k, 1 - b), loc.at[8 + k])
+        if k == 1:
+            return pltpu.make_async_copy(far.at[2 * cx :], c2.at[part], loc.at[9])
+        start = cx * (k // 2)
+        return pltpu.make_async_copy(far.at[start : start + cx], landing(k, 1 - b), loc.at[8 + k])
+
+    share = pltpu.make_async_remote_copy(
+        src_ref=far.at[2 * cx :], dst_ref=c2.at[part],
+        send_sem=red_send.at[4], recv_sem=red_recv.at[4],
+        device_id=(i, other_s), device_id_type=MESH,
+    )
 
     def low_copy(first):
         return pltpu.make_async_copy(first, u.at[1, 0:H, PAD : PAD + ly, :], loc.at[11])
@@ -222,6 +233,7 @@
         pl.semaphore_signal(barrier, inc=1, device_id=(i + 2, s), device_id_type=MESH)
 
     pl.semaphore_wait(barrier, 4 + has_low.astype(jnp.int32) + has_high.astype(jnp.int32))
+    share.start()
 
 
     pieces = ly // PIECE
@@ -397,6 +409,7 @@
         settle(0)
         send_side(1).start()
         settle(1)
+        share.wait()
         for p in order:
             sweep(0, lx, p, square)
         settle(2)
@@ -417,19 +430,16 @@
     band = out.shape[1]
     keep = pl.multiple_of(band * core, 8)
     give = pl.multiple_of(band * (1 - core), 8)
-    swap = pltpu.make_async_remote_copy(
-        src_ref=img.at[:, pl.ds(give, band), :], dst_ref=pair,
-        send_sem=red_send.at[2], recv_sem=red_recv.at[2],
-        device_id=(i, other_s), device_id_type=MESH,
-    )
-    swap.start()
-    swap.wait()
-
-    def add_pair(xi, _):
-        red[xi] = img[xi, pl.ds(keep, band), :] + pair[xi]
-        return 0
-
-    lax.fori_loop(0, lx, add_pair, 0)
+    def swap(half):
+        layers = slice(cx * half, cx * (half + 1))
+        return pltpu.make_async_remote_copy(
+            src_ref=img.at[layers, pl.ds(give, band), :], dst_ref=pair.at[layers],
+            send_sem=red_send.at[2 + half], recv_sem=red_recv.at[2 + half],
+            device_id=(i, other_s), device_id_type=MESH,
+        )
+
+    for half in range(2):
+        swap(half).start()
 
     def deliver(target):
         return pltpu.make_async_remote_copy(
@@ -446,6 +456,9 @@
         )
 
     for target in range(2):
+        swap(target).wait()
+        for xi in range(cx * target, cx * (target + 1)):
+            red[xi] = img[xi, pl.ds(keep, band), :] + pair[xi]
         own = jnp.logical_and(x == b, b == target)
 
         @pl.when(jnp.logical_not(own))
@@ -490,7 +503,9 @@
     def rows_of(block, part):
         return lax.dynamic_slice_in_dim(block, ly * part, ly, 1)
 
-    far = jnp.stack([rows_of(f, 1 - b) for f in (wave_now[0], velocity, wave_prev[0])])
+    core = lax.axis_index("shot") % 2
+    part = lax.dynamic_slice_in_dim(velocity, (cx // 2) * core, cx // 2, 0)
+    far = jnp.concatenate([rows_of(f, 1 - b) for f in (wave_now[0], wave_prev[0], part)])
     far = lax.ppermute(far, "space", swap)
     edge = lax.dynamic_slice_in_dim(wave_now[0], (cx - H) * b, H, 0)
     beyond = [(j, j + 4 * (j % 2) - 2) for j in range(count)]
@@ -569,8 +584,8 @@
             dma((2, cx)),
             dma((13,)),
             dma((steps,)),
-            dma((3,)),
-            dma((3,)),
+            dma((5,)),
+            dma((5,)),
         ],
         compiler_params=pltpu.CompilerParams(
             collective_id=0, has_side_effects=True, vmem_limit_bytes=60 * 2**20

time: 150 us -> 150 us (level)
  waiting for transfers between devices: 7.83 us -> 0.01 us
  local copies, waits for them, and re-layouts: 4.54 us -> 7.6 us
  other arithmetic: 2.72 us -> 5.44 us
    ppermute x1, waiting for transfers between devices: 7.82 us -> 0.01 us  [per_device(): far = lax.ppermute(far, 'space', swap)]
    dynamic_slice x3 -> x4, local copies, waits for them, and re-layouts: 1.21 us -> 4.1 us  [rows_of(): return lax.dynamic_slice_in_dim(block, ly * part, ly, 1)]
    unnamed x24 -> x10, local copies, waits for them, and re-layouts: 3.14 us -> 3.35 us
  transfers between devices with their start and end apart: 5 -> 5, of which waited for: 1 -> 0; matrix products, arithmetic and copies ran while one was open for 2% -> 6% of each run, Pallas kernels for 12% -> 12%
where the time goes in v6:
time: 150 us; the launch traced here: 149 us
  Pallas kernels  126 us (84%)
  starting transfers between devices  9.01 us (6%)
  local copies, waits for them, and re-layouts  7.6 us (5%)
  other arithmetic  5.44 us (4%)
    pallas_call x1, Pallas kernels, per_device(): pl.pallas_call(wave_kernel, out_shape=jax.ShapeDtypeStruct((cx, band, nz)...  108 us
    pallas_call x1, Pallas kernels, per_device(): pl.pallas_call(scatter_kernel, out_shape=(dense, dense, field), in_specs=...  17.9 us
    dynamic_slice x4, local copies, waits for them, and re-layouts, rows_of(): return lax.dynamic_slice_in_dim(block, ly * part, ly, 1)  4.1 us
    ppermute x1, starting transfers between devices, per_device(): same = lax.ppermute(rows_of(edge, b), 'space', within(beyond))  3.49 us
    ppermute x1, starting transfers between devices, per_device(): cross = lax.ppermute(rows_of(edge, 1 - b), 'space', within(across))  3.43 us
    unnamed x10, local copies, waits for them, and re-layouts  3.35 us
  transfers between devices with their start and end apart: 5, of which 0 were waited for; matrix products, arithmetic and copies ran while one was open for 6% of the time, Pallas kernels for 12%

profile of v6, /device:TPU:4, one launch (start us, length us, event | category | flops | bytes accessed | tf_op | source)
XLA Modules:
  0.0 148.8 jit_solution(856596440279359646)
XLA Ops:
  0.7 0.7 fusion.4
  1.3 0.0 collective-permute-start.3
  1.3 0.7 copy.19
  2.1 2.0 %collective-permute-start.4 = (f32[10,512]{1,0:T(8,128)S(1)}, f32[10,512]{1,0:T(8,128)S(1)}, u32[]{:S(2)}, u32[]{:S(2)}) collective-permute-start(f32[10,512]{1,0:T(8,128)S(1)} %bitcast.31), channel_id=1, source_target_pairs={{0,4},{4,0},{8,12},{12,8},{16,20},{20,16},{24,28},{28,24},{1,5},{5... | collective-permute-start | bytes 61448 | tf_op jit(solution)/shard_map/ppermute | solution.py:501
  4.1 1.1 dynamic-slice_bitcast_fusion.2
  5.2 3.4 %collective-permute-start.2 = (f32[4,96,128]{2,1,0:T(8,128)S(1)}, f32[4,96,128]{2,1,0:T(8,128)S(1)}, u32[]{:S(2)}, u32[]{:S(2)}) collective-permute-start(f32[4,96,128]{2,1,0:T(8,128)S(1)} %get-tuple-element.14), channel_id=1, source_target_pairs={{4,8},{8,4},{12,16},{16,12},{20,24},{24,20},{5,9},{9,5},{13,17},{1... | collective-permute-start | bytes 589832 | tf_op jit(solution)/shard_map/ppermute | solution.py:515
  8.6 3.5 %collective-permute-start.1 = (f32[4,96,128]{2,1,0:T(8,128)S(1)}, f32[4,96,128]{2,1,0:T(8,128)S(1)}, u32[]{:S(2)}, u32[]{:S(2)}) collective-permute-start(f32[4,96,128]{2,1,0:T(8,128)S(1)} %get-tuple-element.15), channel_id=1, source_target_pairs={{4,12},{8,0},{12,20},{16,8},{20,28},{24,16},{5,13},{9,1},{13,21},{... | collective-permute-start | bytes 589832 | tf_op jit(solution)/shard_map/ppermute | solution.py:514
  12.1 1.0 dynamic-slice_bitcast_fusion.1
  13.2 1.0 dynamic-slice_bitcast_fusion
  14.2 1.0 constant_dynamic-slice_fusion
  15.2 0.1 pad_maximum_fusion
  15.2 0.1 collective-permute-start
  15.3 0.7 and_select_fusion.7
  16.0 0.7 copy.20
  16.7 0.7 and_select_fusion.5
  17.4 0.1 pad.5.clone
  17.5 0.1 pad.6.clone
  17.6 0.0 collective-permute-done.3
  17.6 0.7 broadcast_select_fusion.1
  18.3 0.1 and_select_fusion.1.enc
  18.3 0.0 collective-permute-done.4
  18.3 0.7 select_bitcast_fusion.1
  19.1 0.1 maximum_maximum_fusion.vals
  19.2 17.9 %scatter.1 = (f32[10,16,96,128]{3,2,1,0:T(8,128)}, f32[10,16,96,128]{3,2,1,0:T(8,128)}, f32[16,96,128]{2,1,0:T(8,128)S(1)}) custom-call(s32[2,512]{1,0:T(2,128)S(1)} %and_select_fusion.1.enc, s32[2,128]{1,0:T(2,128)S(1)} %pad_add_fusion.1.senc, f32[2,16,512]{2,1,0:T(8,128)S(1)} %maximum_maximum_fusion.vals, f32[1,16,128]{2,1,0:T(8,128)S(1)} %maximum_bitcast_fusion.svals), custom_call_target="tpu_custom_call" | custom-call | flops 1000000000 | bytes 80000000 | tf_op jit(solution)/shard_map/scatter/pallas_call | solution.py:545
  37.1 0.0 copy-start
  37.1 0.9 copy-done
  38.0 0.0 collective-permute-done.2.cross
  38.0 0.0 copy-start.2
  38.0 0.0 collective-permute-done.1.same
  38.0 0.0 copy-start.3
  38.0 0.0 collective-permute-done.far
  38.0 0.0 copy-start.1
  38.0 0.6 copy-done.2
  38.6 0.1 copy-done.3
  38.7 0.3 copy-done.1
  39.0 108.0 %waves.1 = f32[8,48,128]{2,1,0:T(8,128)} custom-call(f32[8,192,128]{2,1,0:T(8,128)} %vel.1, f32[1,8,192,128]{3,2,1,0:T(8,128)} %now.1, f32[1,8,192,128]{3,2,1,0:T(8,128)} %prev.1, f32[1,8,192,128]{3,2,1,0:T(8,128)} %adj.1, f32[1,8,192,128]{3,2,1,0:T(8,128)} %adjp.1, f32[20,96,128]{2,1,0:T(8,128)} %copy-done.1, f32[4,96,128]{2,1,0:T(8,128)} %copy-done.3, ...), custom_call_target="tpu_custom_call" | custom-call | tf_op jit(solution)/shard_map/waves/pallas_call | solution.py:566
  147.1 1.7 %fusion.1 = f32[8,48,128]{2,1,0:T(8,128)} fusion(f32[8,48,128]{2,1,0:T(8,128)} %waves.1, f32[8,192,128]{2,1,0:T(8,128)} %vel.1, s32[]{:T(128)S(6)} %select_n.132), kind=kLoop, calls=%fused_computation.5 | loop fusion | flops 196608 | bytes 589828 | tf_op jit(solution)/shard_map/mul | solution.py:596
  (4 shorter events, 0.0 us)
Async XLA Ops:
  1.3 16.2 %collective-permute-start.3 = (s32[512]{0:T(512)S(1)}, s32[512]{0:T(512)S(1)}, u32[]{:S(2)}, u32[]{:S(2)}) collective-permute-start(s32[512]{0:T(512)S(1)} %fusion.4), channel_id=1, source_target_pairs={{0,4},{4,0},{8,12},{12,8},{16,20},{20,16},{24,28},{28,24},{1,5},{5... | collective-permute-start | bytes 6152 | tf_op jit(solution)/shard_map/ppermute | solution.py:500
  2.1 16.3 %collective-permute-start.4 = (f32[10,512]{1,0:T(8,128)S(1)}, f32[10,512]{1,0:T(8,128)S(1)}, u32[]{:S(2)}, u32[]{:S(2)}) collective-permute-start(f32[10,512]{1,0:T(8,128)S(1)} %bitcast.31), channel_id=1, source_target_pairs={{0,4},{4,0},{8,12},{12,8},{16,20},{20,16},{24,28},{28,24},{1,5},{5... | collective-permute-start | bytes 61448 | tf_op jit(solution)/shard_map/ppermute | solution.py:501
  5.2 32.8 %collective-permute-start.2 = (f32[4,96,128]{2,1,0:T(8,128)S(1)}, f32[4,96,128]{2,1,0:T(8,128)S(1)}, u32[]{:S(2)}, u32[]{:S(2)}) collective-permute-start(f32[4,96,128]{2,1,0:T(8,128)S(1)} %get-tuple-element.14), channel_id=1, source_target_pairs={{4,8},{8,4},{12,16},{16,12},{20,24},{24,20},{5,9},{9,5},{13,17},{1... | collective-permute-start | bytes 589832 | tf_op jit(solution)/shard_map/ppermute | solution.py:515
  8.6 29.4 %collective-permute-start.1 = (f32[4,96,128]{2,1,0:T(8,128)S(1)}, f32[4,96,128]{2,1,0:T(8,128)S(1)}, u32[]{:S(2)}, u32[]{:S(2)}) collective-permute-start(f32[4,96,128]{2,1,0:T(8,128)S(1)} %get-tuple-element.15), channel_id=1, source_target_pairs={{4,12},{8,0},{12,20},{16,8},{20,28},{24,16},{5,13},{9,1},{13,21},{... | collective-permute-start | bytes 589832 | tf_op jit(solution)/shard_map/ppermute | solution.py:514
  15.2 22.7 %collective-permute-start = (f32[20,96,128]{2,1,0:T(8,128)S(1)}, f32[20,96,128]{2,1,0:T(8,128)S(1)}, u32[]{:S(2)}, u32[]{:S(2)}) collective-permute-start(f32[20,96,128]{2,1,0:T(8,128)S(1)} %pad_maximum_fusion), channel_id=1, source_target_pairs={{0,4},{4,0},{8,12},{12,8},{16,20},{20,16},{24,28},{28,24},{1,5},{5... | collective-permute-start | bytes 2949128 | tf_op jit(solution)/shard_map/ppermute | solution.py:509
  37.1 0.9 copy-start
  38.0 0.7 copy-start.2
  38.0 0.7 copy-start.3
  38.0 1.1 copy-start.1

commit v7 on v6

--- a/solution.py
+++ b/solution.py
@@ -34,30 +34,39 @@
 
     lax.fori_loop(0, low.shape[0] // 64, clear, 0)
 
-    def place(cells, values, first, tiles):
-        def one(j, _):
+    def place(cells, values, first, tiles, batch):
+        def one(i, _):
             places = []
             for h, table in enumerate((low, high)):
-                cell = cells[h, first + j]
-                line = lax.shift_right_logical(cell, 7)
-                z = cell & 127
-                shift = (z - j) & 127
-                here = lane == z
-                for k, tile in enumerate(tiles):
-                    value = values[h % values.shape[0], 8 * k : 8 * k + 8, first : first + 128]
-                    at = pl.ds(line * TROWS + 8 * tile, 8)
-                    added = jnp.where(here, pltpu.roll(value, shift, 1), 0.0)
-                    places.append((table, at, table[at, :] + added))
+                before = []
+                for n in range(batch):
+                    j = i * batch + n
+                    cell = cells[h, first + j]
+                    line = lax.shift_right_logical(cell, 7)
+                    z = cell & 127
+                    shift = (z - j) & 127
+                    here = lane == z
+                    terms = []
+                    for k, tile in enumerate(tiles):
+                        value = values[h % values.shape[0], 8 * k : 8 * k + 8, first : first + 128]
+                        at = pl.ds(line * TROWS + 8 * tile, 8)
+                        term = jnp.where(here, pltpu.roll(value, shift, 1), 0.0)
+                        terms.append(term)
+                        total = table[at, :] + term
+                        for other, others in before:
+                            total = total + jnp.where(other == line, others[k], 0.0)
+                        places.append((table, at, total))
+                    before.append((line, terms))
             for table, at, value in places:
                 table[at, :] = value
             return 0
 
-        lax.fori_loop(0, 128, one, 0, unroll=8)
+        lax.fori_loop(0, 128 // batch, one, 0, unroll=max(1, 8 // batch))
 
     for first in range(0, slots, 128):
-        place(enc, vals, first, (0, 1))
+        place(enc, vals, first, (0, 1), 4)
     for first in range(0, senc.shape[1], 128):
-        place(senc, svals, first, (1, 2))
+        place(senc, svals, first, (1, 2), 1)
 
     def copies(xi):
         return (

time: 150 us -> 149 us (level)
  no operation moved by 1% of the time
where the time goes in v7:
time: 149 us
  Pallas kernels  126 us (85%)
  starting transfers between devices  9.01 us (6%)
  local copies, waits for them, and re-layouts  7.6 us (5%)
  other arithmetic  5.44 us (4%)
    pallas_call x1, Pallas kernels, per_device(): pl.pallas_call(wave_kernel, out_shape=jax.ShapeDtypeStruct((cx, band, nz)...  108 us
    pallas_call x1, Pallas kernels, per_device(): pl.pallas_call(scatter_kernel, out_shape=(dense, dense, field), in_specs=...  17.6 us
    dynamic_slice x4, local copies, waits for them, and re-layouts, rows_of(): return lax.dynamic_slice_in_dim(block, ly * part, ly, 1)  4.1 us
    ppermute x1, starting transfers between devices, per_device(): same = lax.ppermute(rows_of(edge, b), 'space', within(beyond))  3.49 us
    ppermute x1, starting transfers between devices, per_device(): cross = lax.ppermute(rows_of(edge, 1 - b), 'space', within(across))  3.43 us
    unnamed x10, local copies, waits for them, and re-layouts  3.35 us
  transfers between devices with their start and end apart: 5, of which 0 were waited for; matrix products, arithmetic and copies ran while one was open for 6% of the time, Pallas kernels for 12%

profile of v7, /device:TPU:4, one launch (start us, length us, event | category | flops | bytes accessed | tf_op | source)
XLA Modules:
  0.0 148.6 jit_solution(10137130437735794241)
XLA Ops:
  0.7 0.7 fusion.4
  1.3 0.0 collective-permute-start.3
  1.3 0.7 copy.19
  2.1 2.0 %collective-permute-start.4 = (f32[10,512]{1,0:T(8,128)S(1)}, f32[10,512]{1,0:T(8,128)S(1)}, u32[]{:S(2)}, u32[]{:S(2)}) collective-permute-start(f32[10,512]{1,0:T(8,128)S(1)} %bitcast.31), channel_id=1, source_target_pairs={{0,4},{4,0},{8,12},{12,8},{16,20},{20,16},{24,28},{28,24},{1,5},{5... | collective-permute-start | bytes 61448 | tf_op jit(solution)/shard_map/ppermute | solution.py:510
  4.1 1.1 dynamic-slice_bitcast_fusion.2
  5.2 3.4 %collective-permute-start.2 = (f32[4,96,128]{2,1,0:T(8,128)S(1)}, f32[4,96,128]{2,1,0:T(8,128)S(1)}, u32[]{:S(2)}, u32[]{:S(2)}) collective-permute-start(f32[4,96,128]{2,1,0:T(8,128)S(1)} %get-tuple-element.14), channel_id=1, source_target_pairs={{4,8},{8,4},{12,16},{16,12},{20,24},{24,20},{5,9},{9,5},{13,17},{1... | collective-permute-start | bytes 589832 | tf_op jit(solution)/shard_map/ppermute | solution.py:524
  8.6 3.5 %collective-permute-start.1 = (f32[4,96,128]{2,1,0:T(8,128)S(1)}, f32[4,96,128]{2,1,0:T(8,128)S(1)}, u32[]{:S(2)}, u32[]{:S(2)}) collective-permute-start(f32[4,96,128]{2,1,0:T(8,128)S(1)} %get-tuple-element.15), channel_id=1, source_target_pairs={{4,12},{8,0},{12,20},{16,8},{20,28},{24,16},{5,13},{9,1},{13,21},{... | collective-permute-start | bytes 589832 | tf_op jit(solution)/shard_map/ppermute | solution.py:523
  12.1 1.0 dynamic-slice_bitcast_fusion.1
  13.2 1.0 dynamic-slice_bitcast_fusion
  14.2 1.0 constant_dynamic-slice_fusion
  15.2 0.1 pad_maximum_fusion
  15.2 0.1 collective-permute-start
  15.3 0.7 and_select_fusion.7
  16.0 0.7 copy.20
  16.7 0.7 and_select_fusion.5
  17.4 0.1 pad.5.clone
  17.5 0.1 pad.6.clone
  17.6 0.0 collective-permute-done.3
  17.6 0.7 broadcast_select_fusion.1
  18.3 0.1 and_select_fusion.1.enc
  18.3 0.0 collective-permute-done.4
  18.3 0.7 select_bitcast_fusion.1
  19.1 0.1 maximum_maximum_fusion.vals
  19.2 17.6 %scatter.1 = (f32[10,16,96,128]{3,2,1,0:T(8,128)}, f32[10,16,96,128]{3,2,1,0:T(8,128)}, f32[16,96,128]{2,1,0:T(8,128)S(1)}) custom-call(s32[2,512]{1,0:T(2,128)S(1)} %and_select_fusion.1.enc, s32[2,128]{1,0:T(2,128)S(1)} %pad_add_fusion.1.senc, f32[2,16,512]{2,1,0:T(8,128)S(1)} %maximum_maximum_fusion.vals, f32[1,16,128]{2,1,0:T(8,128)S(1)} %maximum_bitcast_fusion.svals), custom_call_target="tpu_custom_call" | custom-call | flops 1000000000 | bytes 80000000 | tf_op jit(solution)/shard_map/scatter/pallas_call | solution.py:554
  36.8 0.0 copy-start
  36.8 0.9 copy-done
  37.7 0.0 collective-permute-done.2.cross
  37.7 0.0 copy-start.2
  37.7 0.0 collective-permute-done.1.same
  37.7 0.0 copy-start.3
  37.7 0.0 collective-permute-done.far
  37.7 0.0 copy-start.1
  37.7 0.6 copy-done.2
  38.4 0.1 copy-done.3
  38.4 0.3 copy-done.1
  38.8 108.1 %waves.1 = f32[8,48,128]{2,1,0:T(8,128)} custom-call(f32[8,192,128]{2,1,0:T(8,128)} %vel.1, f32[1,8,192,128]{3,2,1,0:T(8,128)} %now.1, f32[1,8,192,128]{3,2,1,0:T(8,128)} %prev.1, f32[1,8,192,128]{3,2,1,0:T(8,128)} %adj.1, f32[1,8,192,128]{3,2,1,0:T(8,128)} %adjp.1, f32[20,96,128]{2,1,0:T(8,128)} %copy-done.1, f32[4,96,128]{2,1,0:T(8,128)} %copy-done.3, ...), custom_call_target="tpu_custom_call" | custom-call | tf_op jit(solution)/shard_map/waves/pallas_call | solution.py:575
  146.9 1.7 %fusion.1 = f32[8,48,128]{2,1,0:T(8,128)} fusion(f32[8,48,128]{2,1,0:T(8,128)} %waves.1, f32[8,192,128]{2,1,0:T(8,128)} %vel.1, s32[]{:T(128)S(6)} %select_n.132), kind=kLoop, calls=%fused_computation.5 | loop fusion | flops 196608 | bytes 589828 | tf_op jit(solution)/shard_map/mul | solution.py:605
  (4 shorter events, 0.0 us)
Async XLA Ops:
  1.3 16.2 %collective-permute-start.3 = (s32[512]{0:T(512)S(1)}, s32[512]{0:T(512)S(1)}, u32[]{:S(2)}, u32[]{:S(2)}) collective-permute-start(s32[512]{0:T(512)S(1)} %fusion.4), channel_id=1, source_target_pairs={{0,4},{4,0},{8,12},{12,8},{16,20},{20,16},{24,28},{28,24},{1,5},{5... | collective-permute-start | bytes 6152 | tf_op jit(solution)/shard_map/ppermute | solution.py:509
  2.1 16.3 %collective-permute-start.4 = (f32[10,512]{1,0:T(8,128)S(1)}, f32[10,512]{1,0:T(8,128)S(1)}, u32[]{:S(2)}, u32[]{:S(2)}) collective-permute-start(f32[10,512]{1,0:T(8,128)S(1)} %bitcast.31), channel_id=1, source_target_pairs={{0,4},{4,0},{8,12},{12,8},{16,20},{20,16},{24,28},{28,24},{1,5},{5... | collective-permute-start | bytes 61448 | tf_op jit(solution)/shard_map/ppermute | solution.py:510
  5.2 32.5 %collective-permute-start.2 = (f32[4,96,128]{2,1,0:T(8,128)S(1)}, f32[4,96,128]{2,1,0:T(8,128)S(1)}, u32[]{:S(2)}, u32[]{:S(2)}) collective-permute-start(f32[4,96,128]{2,1,0:T(8,128)S(1)} %get-tuple-element.14), channel_id=1, source_target_pairs={{4,8},{8,4},{12,16},{16,12},{20,24},{24,20},{5,9},{9,5},{13,17},{1... | collective-permute-start | bytes 589832 | tf_op jit(solution)/shard_map/ppermute | solution.py:524
  8.6 29.1 %collective-permute-start.1 = (f32[4,96,128]{2,1,0:T(8,128)S(1)}, f32[4,96,128]{2,1,0:T(8,128)S(1)}, u32[]{:S(2)}, u32[]{:S(2)}) collective-permute-start(f32[4,96,128]{2,1,0:T(8,128)S(1)} %get-tuple-element.15), channel_id=1, source_target_pairs={{4,12},{8,0},{12,20},{16,8},{20,28},{24,16},{5,13},{9,1},{13,21},{... | collective-permute-start | bytes 589832 | tf_op jit(solution)/shard_map/ppermute | solution.py:523
  15.2 22.5 %collective-permute-start = (f32[20,96,128]{2,1,0:T(8,128)S(1)}, f32[20,96,128]{2,1,0:T(8,128)S(1)}, u32[]{:S(2)}, u32[]{:S(2)}) collective-permute-start(f32[20,96,128]{2,1,0:T(8,128)S(1)} %pad_maximum_fusion), channel_id=1, source_target_pairs={{0,4},{4,0},{8,12},{12,8},{16,20},{20,16},{24,28},{28,24},{1,5},{5... | collective-permute-start | bytes 2949128 | tf_op jit(solution)/shard_map/ppermute | solution.py:518
  36.8 0.9 copy-start
  37.7 0.7 copy-start.2
  37.7 0.7 copy-start.3
  37.7 1.1 copy-start.1
